TPU v7x, 32 devices: a whole 2x2x4 slice. The times are simulated.
32 devices in a mesh: ctx: 4 (over y, x), exp: 8 (over z, core).
Axes of the slice: x: 2, y: 2, z: 4, core: 2. Of those that a mesh axis runs over, the one named last changes fastest.
Arguments:
- tokens: bfloat16 [8, 1024, 1536], P('exp', 'ctx'), may hold values from -6 to 6
- routes: int32 [8, 1024, 4], P('exp', 'ctx'), may hold values from 0 to 15, all different within a row; in each aligned block of 256 rows (0 to 255, 256 to 511, ..., all dimensions but the last counted through in order) at most 128 rows name the same one
- gain_attn: bfloat16 [1536], P('exp'), may hold values from 0.5 to 1.5
- w_query: bfloat16 [1536, 1536], P('exp'), may hold values from -0.15625 to 0.15625
- key_value_weight: bfloat16 [1536, 512], P('exp'), may hold values from -0.15625 to 0.15625
- w_out: bfloat16 [1536, 1536], P('exp'), may hold values from -3.5 to 3.5
- gain_ffn: bfloat16 [1536], P('exp'), may hold values from 0.5 to 1.5
- w_router: bfloat16 [1536, 16], P('exp'), may hold values from -0.078125 to 0.078125
- w_gate: bfloat16 [16, 1536, 768], P('exp'), may hold values from -0.15625 to 0.15625
- w_up: bfloat16 [16, 1536, 768], P('exp'), may hold values from -0.15625 to 0.15625
- w_down: bfloat16 [16, 768, 1536], P('exp'), may hold values from -0.4375 to 0.4375
- cotangent: bfloat16 [8, 1024, 1536], P('exp', 'ctx'), may hold values from -6 to 6
Outputs:
- output: bfloat16 [8, 1024, 1536], P('exp', 'ctx')
- grad_tokens: float32 [8, 1024, 1536], P('exp', 'ctx')
- grad_gain_attn: float32 [1536], P('exp')
- grad_query: float32 [1536, 1536], P('exp')
- grad_keyval: float32 [1536, 512], P('exp')
- grad_out: float32 [1536, 1536], P('exp')
- grad_gain_ffn: float32 [1536], P('exp')
- grad_router: float32 [1536, 16], P('exp')
- grad_gate: float32 [16, 1536, 768], P('exp')
- grad_up: float32 [16, 1536, 768], P('exp')
- grad_down: float32 [16, 768, 1536], P('exp')
Inputs may be any that keep to these rules, and one draw needn't show every extreme that they name: `routes`: each token names 4 different experts. In the 256 tokens of one device (aligned blocks along a sequence) no expert is named by more than 128 tokens, a bound that some block reaches.
All inputs are finite; a program needn't handle non-finite values.
Results may differ from a plain program's by a relative error of at most 0.025.
Values may be sent and summed in bfloat16 or wider, within the bound.
A program may use at most 192 MiB of HBM per device.

v0:
```python
import functools
import math

import jax
import jax.numpy as jnp
from jax import lax
from jax.experimental import pallas as pl
from jax.experimental.pallas import tpu as pltpu
from jax.sharding import PartitionSpec as P

MESH = pl.DeviceIdType.MESH
ANY = pl.BlockSpec(memory_space=pl.ANY)


def remote(src, dst, send, recv, ctx, exp):
    return pltpu.make_async_remote_copy(
        src_ref=src, dst_ref=dst, send_sem=send, recv_sem=recv, device_id=(ctx, exp), device_id_type=MESH
    )


def greet(pairs):
    barrier = pltpu.get_barrier_semaphore()
    count = 0
    for here, ctx, exp in pairs:
        if here is True:
            pl.semaphore_signal(barrier, inc=1, device_id=(ctx, exp), device_id_type=MESH)
            count = count + 1
        else:
            @pl.when(here)
            def _():
                pl.semaphore_signal(barrier, inc=1, device_id=(ctx, exp), device_id_type=MESH)
            count = count + here.astype(jnp.int32)
    pl.semaphore_wait(barrier, count)


QUERY_HEADS = 12
KEY_VALUE_HEADS = 2
HEAD_WIDTH = 128
EPS = 1e-06
NEG = -1e30
ROPE_BASE = 1000000.0


class Gathering:
    def __init__(self, line, own, out, sems, keep_own=True, window=None):
        self.line, self.keep_own = line, keep_own
        self.window = pl.ds(*window) if window is not None else pl.ds(0, out.shape[1])
        self.own, self.whole = own.at[self.window], out
        self.local_sem, self.z_send, self.z_recv, self.c_send, self.c_recv = sems
        self.c, self.e = lax.axis_index("ctx"), lax.axis_index("exp")
        self.p, self.k = self.e // 2, self.e % 2

    def block(self, q):
        return self.whole.at[2 * q + self.k, self.window]

    def along(self, q, src, to_right):
        there = self.e + 2 if to_right else self.e - 2
        way = 0 if to_right else 1
        return remote(src, self.block(q), self.z_send.at[way, q], self.z_recv.at[q], self.c, there)

    def across(self, q, src):
        there = self.e + 1 - 2 * self.k
        return remote(src, self.block(q), self.c_send.at[q], self.c_recv.at[q], self.c, there)

    def local(self):
        return pltpu.make_async_copy(self.own, self.whole.at[self.e, self.window], self.local_sem)

    def ends(self, d):
        for to_right in (True, False):
            q = self.p - d if to_right else self.p + d
            here = (q >= 0) if to_right else (q < self.line)
            further = (self.p < self.line - 1) if to_right else (self.p > 0)
            yield to_right, q, here, further

    def begin(self):
        for to_right, q, _, further in self.ends(0):
            @pl.when(further)
            def _():
                self.along(q, self.own, to_right).start()

        self.across(self.p, self.own).start()
        if self.keep_own:
            self.local().start()

    def pump(self, d, onward=True):
        for to_right, q, here, further in self.ends(d):
            @pl.when(here)
            def _():
                block = self.block(q)
                self.along(q, block, to_right).wait_recv()
                if onward:
                    @pl.when(further)
                    def _():
                        self.along(q, block, to_right).start()

                self.across(q, block).start()

    def forward(self, d):
        for to_right, q, here, further in self.ends(d):
            @pl.when(here & further)
            def _():
                self.along(q, self.block(q), to_right).start()

    def finish(self, sent, crossed):
        for d in crossed:
            for to_right, q, here, _ in self.ends(d):
                if d > 0 or to_right:
                    @pl.when(here)
                    def _():
                        self.across(q, self.own).wait()
        for d in sent:
            for to_right, q, here, further in self.ends(d):
                @pl.when(here & further)
                def _():
                    self.along(q, self.own, to_right).wait_send()

    def end(self, hops=None):
        last = self.line if hops is None else min(self.line, hops + 1)
        if self.keep_own:
            self.local().wait()
        self.finish(range(self.line if hops is None else last - 1), range(last))

    @staticmethod
    def scratch(line):
        dma = pltpu.SemaphoreType.DMA
        return [dma, dma((2, line)), dma((line,)), dma((line,)), dma((line,))]


def gather_kernel(line, own, out, *sems):
    c, e = lax.axis_index("ctx"), lax.axis_index("exp")
    greet([(e >= 2, c, e - 2), (e < 2 * line - 2, c, e + 2), (True, c, e + 1 - 2 * (e % 2))])
    gathering = Gathering(line, own, out, sems)
    gathering.begin()
    for d in range(1, line):
        gathering.pump(d)
    gathering.end()


def gather_rows(own, collective_id):
    n = lax.axis_size("exp")
    return pl.pallas_call(
        functools.partial(gather_kernel, n // 2),
        out_shape=jax.ShapeDtypeStruct((n,) + own.shape, own.dtype),
        in_specs=[ANY],
        out_specs=ANY,
        scratch_shapes=Gathering.scratch(n // 2),
        compiler_params=pltpu.CompilerParams(collective_id=collective_id, has_side_effects=True),
        name="gather_rows",
    )(own)


def add_rows(dst, a, b, rows):
    step = math.gcd(rows, 64)

    def body(i, carried):
        at = pl.ds(pl.multiple_of(i * step, step), step)
        dst[at, :] = a[at, :] + b[at, :]
        return carried

    lax.fori_loop(0, rows // step, body, 0)


class Summing:
    def __init__(self, line, part, cross, moving, acc, tmp, sems):
        self.line, self.part, self.cross, self.moving = line, part, cross, moving
        self.acc, self.tmp = acc, tmp
        self.own_sem, self.tmp_sem, self.c_send, self.c_recv, self.z_send, self.z_recv = sems
        self.c, self.e = lax.axis_index("ctx"), lax.axis_index("exp")
        self.p, self.k = self.e // 2, self.e % 2
        self.rows, self.width = part.shape[1:]

    def across(self, q):
        there = self.e + 1 - 2 * self.k
        return remote(
            self.part.at[2 * q + 1 - self.k], self.cross.at[q], self.c_send.at[q], self.c_recv.at[q], self.c, there
        )

    def own(self, q):
        return pltpu.make_async_copy(self.part.at[2 * q + self.k], self.acc.at[q], self.own_sem.at[q])

    def load(self, src, side):
        into = self.tmp.at[side, pl.ds(0, self.rows), pl.ds(0, self.width)]
        return pltpu.make_async_copy(src, into, self.tmp_sem.at[side])

    def add(self, q, side):
        add_rows(self.acc.at[q], self.acc.at[q], self.tmp.at[side, pl.ds(0, self.rows), pl.ds(0, self.width)], self.rows)

    def along(self, q, to_right):
        there = self.e + 2 if to_right else self.e - 2
        place = q if to_right else jnp.where(q == self.p - 1, self.line, q)
        return remote(self.acc.at[q], self.moving.at[place], self.z_send.at[q], self.z_recv.at[place], self.c, there)

    def arrived(self, place):
        return remote(self.acc.at[0], self.moving.at[place], self.z_send.at[0], self.z_recv.at[place], self.c, self.e)

    def ends(self, d):
        for to_right in (True, False):
            if d > 0 or to_right:
                q = self.p + d if to_right else self.p - d
                here = (q < self.line) if to_right else (q >= 0)
                yield to_right, q, here, ((self.p > 0) if to_right else (self.p < self.line - 1))

    def begin(self):
        order = [(d, end) for d in range(self.line - 1, -1, -1) for end in self.ends(d)]
        for _, (_, q, here, _) in order:
            @pl.when(here)
            def _():
                self.across(q).start()
                self.own(q).start()
        for d, (to_right, q, here, behind) in order:
            side = 0 if to_right else 1

            @pl.when(here)
            def _():
                self.across(q).wait_recv()
                self.load(self.cross.at[q], side).start()
                self.own(q).wait()
                self.load(self.cross.at[q], side).wait()
                self.add(q, side)
                if d > 0:
                    @pl.when(jnp.logical_not(behind))
                    def _():
                        self.along(q, to_right).start()

    def step(self, d):
        if d > 0:
            for to_right, q, here, behind in self.ends(d):
                @pl.when(here & behind)
                def _():
                    self.arrived(q).wait_recv()
                    self.load(self.moving.at[q], 0 if to_right else 1).start()
            for to_right, q, here, behind in self.ends(d):
                @pl.when(here & behind)
                def _():
                    side = 0 if to_right else 1
                    self.load(self.moving.at[q], side).wait()
                    self.add(q, side)
                    self.along(q, to_right).start()
            return
        last = ((0, self.p, self.p > 0), (1, self.line, self.p < self.line - 1))
        for side, place, behind in last:
            @pl.when(behind)
            def _():
                self.arrived(place).wait_recv()
                self.load(self.moving.at[place], side).start()
        for side, place, behind in last:
            @pl.when(behind)
            def _():
                self.load(self.moving.at[place], side).wait()
                self.add(self.p, side)

    def result(self):
        return self.acc.at[self.p]

    def end(self):
        for d in range(self.line):
            for to_right, q, here, _ in self.ends(d):
                @pl.when(here)
                def _():
                    if d > 0:
                        self.along(q, to_right).wait_send()
                    self.across(q).wait_send()

    @staticmethod
    def scratch(line, rows, width):
        dma = pltpu.SemaphoreType.DMA
        return [
            pltpu.VMEM((line, rows, width), jnp.bfloat16),
            dma((line,)),
            dma((2,)),
            dma((line,)),
            dma((line,)),
            dma((line,)),
            dma((line + 1,)),
        ]

    @staticmethod
    def landing(line, rows, width):
        return [
            jax.ShapeDtypeStruct((line, rows, width), jnp.bfloat16),
            jax.ShapeDtypeStruct((line + 1, rows, width), jnp.bfloat16),
        ]


class Totals:
    ahead, lag, count, early = 4, 1, 12, 4

    def __init__(self, part, early_first, sends, recvs, total=None, first=None, second=None, buffers=None, sems=None):
        self.part, self.total, self.early_first, self.first, self.second = part, total, early_first, first, second
        self.sends, self.recvs = sends, recvs
        if buffers is not None:
            self.own, self.got, self.got_two = buffers
            self.load_sem, self.got_sem, self.store_sem = sems
            self.slots = self.own.shape[0]
        c, self.e = lax.axis_index("ctx"), lax.axis_index("exp")
        self.bits = (c % 2, c // 2)
        self.nbrs = (c + 1 - 2 * (c % 2), lax.rem(c + 2, 4))
        self.deep = part.shape[0] // self.count

    def axes(self, h):
        return (0, 1) if h == 0 else (1, 0)

    def rows(self, ref, t, h, kept_one, kept_two=None, mine_two=True):
        one, two = self.axes(h)
        quarter, eighth = self.deep // 4, self.deep // 8
        bit = self.bits[one] if kept_one else 1 - self.bits[one]
        start = t * self.deep + h * (self.deep // 2) + bit * quarter
        if kept_two is None:
            return ref.at[pl.ds(pl.multiple_of(start, 16), quarter), :]
        return ref.at[pl.ds(pl.multiple_of(start + self.bits[two] * eighth, 16), eighth), :]

    def piece(self, t, h, kept):
        eighth = self.deep // 8
        bit = self.bits[self.axes(h)[1]]
        start = (bit if kept else 1 - bit) * eighth
        return self.own.at[t % self.slots, h, pl.ds(pl.multiple_of(start, 16), eighth), :]

    def copy(self, stage, t, h):
        one, two = self.axes(h)
        if stage == 0:
            src, dst, there = self.rows(self.part, t, h, False), self.landed(t, h), one
        elif stage == 1:
            src, dst, there = self.piece(t, h, False), self.second.at[t, h], two
        elif stage == 2:
            src, dst, there = self.piece(t, h, True), self.rows(self.total, t, h, True, True), two
        else:
            src, dst, there = self.rows(self.total, t, h, True), self.rows(self.total, t, h, True), one
        return remote(src, dst, self.sends.at[stage, t, h], self.recvs.at[stage, t, h], self.nbrs[there], self.e)

    def landed(self, t, h):
        return self.early_first.at[t, h] if t < self.early else self.first.at[t - self.early, h]

    def start_early(self, t):
        for h in range(2):
            self.copy(0, t, h).start()

    def end_early(self):
        for t in range(self.early):
            for h in range(2):
                self.copy(0, t, h).wait()

    def load_own(self, t, h):
        return pltpu.make_async_copy(
            self.rows(self.part, t, h, True), self.own.at[t % self.slots, h], self.load_sem.at[t % 2, h]
        )

    def store(self, t, h):
        return pltpu.make_async_copy(
            self.piece(t, h, True), self.rows(self.total, t, h, True, True), self.store_sem.at[t % self.slots, h]
        )

    def begin(self):
        for t in range(self.early, min(self.early + self.ahead, self.count)):
            for h in range(2):
                self.copy(0, t, h).start()
        for h in range(2):
            self.load_own(0, h).start()

    @property
    def ticks(self):
        return self.count + 2 * self.lag

    def tick(self, t):
        count, lag = self.count, self.lag
        t_two, t_three = t - lag, t - 2 * lag
        loads = []
        if t < count:
            for h in range(2):
                if t >= self.early:
                    self.copy(0, t, h).wait_recv()
                came = pltpu.make_async_copy(self.landed(t, h), self.got.at[h], self.got_sem.at[0, h])
                came.start()
                loads.append(came)
            if t + self.early + self.ahead < count:
                for h in range(2):
                    self.copy(0, t + self.early + self.ahead, h).start()
        later = []
        if 0 <= t_two < count:
            for h in range(2):
                self.copy(1, t_two, h).wait_recv()
                came = pltpu.make_async_copy(self.second.at[t_two, h], self.got_two.at[h], self.got_sem.at[1, h])
                came.start()
                later.append(came)
        if t < count:
            for h in range(2):
                self.load_own(t, h).wait()
                loads[h].wait()
                mine = self.own.at[t % self.slots, h]
                add_rows(mine, mine, self.got.at[h], self.deep // 4)
                self.copy(1, t, h).start()
        if 0 <= t_two < count:
            for h in range(2):
                later[h].wait()
                mine = self.piece(t_two, h, True)
                add_rows(mine, mine, self.got_two.at[h], self.deep // 8)
                self.copy(2, t_two, h).start()
                self.store(t_two, h).start()
        if 0 <= t_three < count:
            for h in range(2):
                self.copy(2, t_three, h).wait_recv()
                self.store(t_three, h).wait()
                self.copy(3, t_three, h).start()
                self.copy(1, t_three, h).wait_send()
                self.copy(2, t_three, h).wait_send()
        if t + 1 < count:
            for h in range(2):
                self.load_own(t + 1, h).start()

    def end(self):
        for t in range(self.count):
            for h in range(2):
                if t >= self.early:
                    self.copy(0, t, h).wait_send()
                self.copy(3, t, h).wait()

    @staticmethod
    def early_scratch():
        dma = pltpu.SemaphoreType.DMA
        return [dma((1, Totals.early, 2)), dma((1, Totals.early, 2))]

    @staticmethod
    def early_landing(deep, width):
        return jax.ShapeDtypeStruct((Totals.early, 2, deep // 4, width), jnp.bfloat16)

    @staticmethod
    def scratch(deep, width):
        count = Totals.count
        dma = pltpu.SemaphoreType.DMA
        slots = 2 * Totals.lag + 1
        return [
            pltpu.VMEM((slots, 2, deep // 4, width), jnp.bfloat16),
            pltpu.VMEM((2, deep // 4, width), jnp.bfloat16),
            pltpu.VMEM((2, deep // 8, width), jnp.bfloat16),
            dma((4, count, 2)),
            dma((4, count, 2)),
            dma((2, 2)),
            dma((2, 2)),
            dma((slots, 2)),
        ]

    @staticmethod
    def landing(deep, width):
        return [
            jax.ShapeDtypeStruct((Totals.count - Totals.early, 2, deep // 4, width), jnp.bfloat16),
            jax.ShapeDtypeStruct((Totals.count, 2, deep // 8, width), jnp.bfloat16),
        ]


class Sharing:
    def __init__(self, size, part, total, summed, arrived, sems):
        self.size, self.part, self.total, self.summed, self.arrived_at = size, part, total, summed, arrived
        self.a_send, self.a_recv, self.b_send, self.b_recv, self.store_sem = sems
        self.c, self.e = lax.axis_index("ctx"), lax.axis_index("exp")
        self.piece = part.shape[0] // size

    def rows(self, ref, j):
        return ref.at[pl.ds(pl.multiple_of(j * self.piece, 16), self.piece), :]

    def there(self, i):
        return lax.rem(self.c + i + 1, self.size)

    def give(self, i):
        there = self.there(i)
        return remote(
            self.rows(self.part, there), self.arrived_at.at[i], self.a_send.at[i], self.a_recv.at[i], there, self.e
        )

    def hand(self, i):
        return remote(
            self.summed, self.rows(self.total, self.c), self.b_send.at[i], self.b_recv.at[i], self.there(i), self.e
        )

    def handed(self, i):
        source = lax.rem(self.c + self.size - 1 - i, self.size)
        return remote(
            self.summed, self.rows(self.total, source), self.b_send.at[i], self.b_recv.at[i], self.there(i), self.e
        )

    def store(self):
        return pltpu.make_async_copy(self.summed, self.rows(self.total, self.c), self.store_sem)

    def begin(self):
        for i in range(self.size - 1):
            self.give(i).start()

    def middle(self):
        for i in range(self.size - 1):
            self.give(i).wait_recv()
        for j in range(self.piece // 16):
            at = pl.ds(j * 16, 16)
            total = self.part[pl.ds(pl.multiple_of(self.c * self.piece + j * 16, 16), 16), :].astype(jnp.float32)
            for i in range(self.size - 1):
                total = total + self.arrived_at[i, at, :].astype(jnp.float32)
            self.summed[at, :] = total.astype(self.summed.dtype)
        for i in range(self.size - 1):
            self.hand(i).start()
        self.store().start()

    def end(self):
        self.store().wait()
        for i in range(self.size - 1):
            self.give(i).wait_send()
            self.hand(i).wait_send()
            self.handed(i).wait_recv()

    @staticmethod
    def scratch(size, rows, width):
        dma = pltpu.SemaphoreType.DMA
        return [
            pltpu.VMEM((rows // size, width), jnp.bfloat16),
            pltpu.VMEM((size - 1, rows // size, width), jnp.bfloat16),
            dma((size - 1,)),
            dma((size - 1,)),
            dma((size - 1,)),
            dma((size - 1,)),
            dma,
        ]


def weights_kernel(line, quarter, *refs):
    count = 3
    own, own_mask, own_block = refs[:count], refs[count], refs[count + 1]
    out, masks, blocks = refs[count + 2 : 2 * count + 2], refs[2 * count + 2], refs[2 * count + 3]
    held, refs = refs[2 * count + 4 : 3 * count + 4], refs[3 * count + 4 :]
    local_sem, own_send, own_recv, z_send, z_recv, xy_send, xy_recv, d_send, d_recv, c_send, c_recv = refs[:-10]
    c, e = lax.axis_index("ctx"), lax.axis_index("exp")
    p, k = e // 2, e % 2
    sibling = e + 1 - 2 * k
    rows = own[0].shape[0]
    nbr = (c + 1 - 2 * (c % 2), (c + 2) % 4)
    opposite = 3 - c
    greet(
        [
            (p > 0, c, e - 2),
            (p < line - 1, c, e + 2),
            (True, c, sibling),
            (True, nbr[0], e),
            (True, nbr[1], e),
        ]
    )

    def whole(a):
        return out[a].at[pl.ds(pl.multiple_of(e * rows, 16), rows), :]

    def piece(a, q, column):
        return out[a].at[pl.ds(pl.multiple_of((2 * q + k) * rows + column * quarter, 16), quarter), :]

    def own_piece(a):
        return own[a].at[pl.ds(pl.multiple_of(c * quarter, 16), quarter), :]

    def load(a):
        return pltpu.make_async_copy(own[a], held[a], local_sem.at[0, a])

    def local(a):
        return pltpu.make_async_copy(held[a], whole(a), local_sem.at[1, a])

    def own_across(a):
        return remote(own[a], whole(a), own_send.at[a], own_recv.at[a], c, sibling)

    def along(a, q, src, to_right):
        there = e + 2 if to_right else e - 2
        way = 0 if to_right else 1
        return remote(src, piece(a, q, c), z_send.at[way, q, a], z_recv.at[q, a], c, there)

    def beside(a, q, axis):
        return remote(piece(a, q, c), piece(a, q, c), xy_send.at[axis, q, a], xy_recv.at[axis, q, a], nbr[axis], e)

    def onward(a, q):
        came, goes = (0, 1) if a == 0 else (1, 0)
        block = piece(a, q, nbr[came])
        return remote(block, block, d_send.at[q, a], d_recv.at[q, a], nbr[goes], e)

    def across(a, q, j):
        column = (c, nbr[0], nbr[1], opposite)[j]
        block = piece(a, q, column)
        return remote(block, block, c_send.at[q, j, a], c_recv.at[q, j, a], c, sibling)

    arrays = range(count)
    marking = Gathering(line, own_mask, masks, refs[-10:-5])
    gathering = Gathering(line, own_block, blocks, refs[-5:], keep_own=False)
    marking.begin()
    for a in arrays:
        @pl.when(p < line - 1)
        def _():
            along(a, p, own_piece(a), True).start()

        @pl.when(p > 0)
        def _():
            along(a, p, own_piece(a), False).start()
    for a in arrays:
        own_across(a).start()
        load(a).start()
    for a in arrays:
        load(a).wait()
        local(a).start()

    def ends(d):
        for to_right in (True, False):
            q = p - d if to_right else p + d
            yield to_right, q, ((q >= 0) if to_right else (q < line))

    for d in range(1, line + 1):
        if d < line:
            for to_right, q, here in ends(d):
                further = (p < line - 1) if to_right else (p > 0)

                @pl.when(here)
                def _():
                    for a in arrays:
                        along(a, q, piece(a, q, c), to_right).wait_recv()

                        @pl.when(further)
                        def _():
                            along(a, q, piece(a, q, c), to_right).start()

                        beside(a, q, 0).start()
                        beside(a, q, 1).start()
                        across(a, q, 0).start()
        if d < line:
            marking.pump(d)
        if d == line - 1:
            gathering.begin()
        if d > 1:
            for to_right, q, here in ends(d - 1):
                @pl.when(here)
                def _():
                    for a in arrays:
                        came = 0 if a == 0 else 1
                        beside(a, q, came).wait_recv()
                        onward(a, q).start()
                        across(a, q, 1 + came).start()
                        beside(a, q, 1 - came).wait_recv()
                        across(a, q, 2 - came).start()
    for d in range(1, line):
        for to_right, q, here in ends(d):
            @pl.when(here)
            def _():
                for a in arrays:
                    onward(a, q).wait_recv()
                    across(a, q, 3).start()
    gathering.pump(1, onward=False)
    gathering.end(1)
    marking.end()
    for a in arrays:
        local(a).wait()
        own_across(a).wait()
    for d in range(0, line):
        for to_right, q, here in ends(d):
            further = (p < line - 1) if to_right else (p > 0)
            for a in arrays:
                @pl.when(here & further)
                def _():
                    along(a, q, piece(a, q, c), to_right).wait_send()
                if d > 0:
                    @pl.when(here)
                    def _():
                        beside(a, q, 0).wait_send()
                        beside(a, q, 1).wait_send()
                        onward(a, q).wait_send()
                        for j in range(4):
                            across(a, q, j).wait()


def planned(size, n, shard_rows):
    return size == 4 and n in (4, 6, 8) and (shard_rows // 4) % 16 == 0


def gather_weights(shards, mask, block, collective_id):
    n = lax.axis_size("exp")
    if not planned(lax.axis_size("ctx"), n, shards[0].shape[0]):
        whole = tuple(lax.all_gather(w, "exp", axis=0, tiled=True) for w in shards)
        return whole + (lax.all_gather(mask, "exp", axis=0), gather_rows(block, collective_id))
    line = n // 2
    count = len(shards)
    dma = pltpu.SemaphoreType.DMA
    return pl.pallas_call(
        functools.partial(weights_kernel, line, shards[0].shape[0] // 4),
        out_shape=tuple(jax.ShapeDtypeStruct((n * w.shape[0], w.shape[1]), w.dtype) for w in shards)
        + tuple(jax.ShapeDtypeStruct((n,) + w.shape, w.dtype) for w in (mask, block)),
        in_specs=[ANY] * (count + 2),
        out_specs=(ANY,) * (count + 2),
        scratch_shapes=[pltpu.VMEM(w.shape, w.dtype) for w in shards]
        + [
            dma((2, count)),
            dma((count,)),
            dma((count,)),
            dma((2, line, count)),
            dma((line, count)),
            dma((2, line, count)),
            dma((2, line, count)),
            dma((line, count)),
            dma((line, count)),
            dma((line, 4, count)),
            dma((line, 4, count)),
        ]
        + Gathering.scratch(line)
        + Gathering.scratch(line),
        compiler_params=pltpu.CompilerParams(
            collective_id=collective_id, has_side_effects=True, vmem_limit_bytes=62 << 20
        ),
        name="gather_weights",
    )(*shards, mask, block)


def dot(a, b):
    return lax.dot_general(a, b, (((1,), (0,)), ((), ())), preferred_element_type=jnp.float32)


def dot_nt(a, b):
    return lax.dot_general(a, b, (((1,), (1,)), ((), ())), preferred_element_type=jnp.float32)


def dot_tn(a, b):
    return lax.dot_general(a, b, (((0,), (0,)), ((), ())), preferred_element_type=jnp.float32)


def visit(p, line, i):
    both = jnp.minimum(p, line - 1 - p)
    d = jnp.where(i <= 2 * both, (i + 1) // 2, i - both)
    left = jnp.where(i <= 2 * both, i % 2 == 1, p > line - 1 - p)
    q = jnp.where(left, p - d, p + d)
    first = (i == 0) | (i > 2 * both) | (i % 2 == 1)
    return q, d, first


def expert_kernel(line, local, cap, hop, start, hidden, own_grads, grads_in, named, router, w_gate, w_up, w_down, *refs):
    hidden_all, out_part, back_part, grads, grads_all = refs[:5]
    if start:
        early_first, refs = refs[5], refs[:5] + refs[6:]
    wg, wu, wd, xs, ds, act, dg, du, es, h_buf, y_buf, out_stage, back_stage, in_stage, down_stage = refs[5:20]
    picks, xs_turned, act_turned, gate_kept, refs = *refs[20:24], refs[:20] + refs[24:]
    w_sem, own_sem, z_send, z_recv, c_send, c_recv, h_sem, y_sem, o_sem, b_sem, s_sem = refs[20:31]
    f32, bf16 = jnp.float32, jnp.bfloat16
    c, e = lax.axis_index("ctx"), lax.axis_index("exp")
    p, k = e // 2, e % 2
    sibling = e + 1 - 2 * k
    rows, width = hidden.shape
    hidden_units = wg.shape[2]
    slots = 2 * cap
    lanes = router.shape[1]

    loads = [
        pltpu.make_async_copy(src, dst, w_sem.at[i])
        for i, (src, dst) in enumerate(((w_gate, wg), (w_up, wu), (w_down, wd)))
    ]
    for copy in loads:
        copy.start()
    beside = [(True, c + 1 - 2 * (c % 2), e), (True, lax.rem(c + 2, 4), e)] if start else []
    greet([(p > 0, c, e - 2), (p < line - 1, c, e + 2), (True, c, sibling)] + beside)
    def along(q, src, to_right):
        there = e + 2 if to_right else e - 2
        return remote(src, hidden_all.at[2 * q + k], z_send.at[0 if to_right else 1, q], z_recv.at[q], c, there)

    def across(q, src):
        return remote(src, hidden_all.at[2 * q + k], c_send.at[q], c_recv.at[q], c, sibling)

    def load_hidden(q, slot):
        return pltpu.make_async_copy(hidden_all.at[pl.ds(2 * q, 2)], h_buf.at[slot], h_sem.at[slot])

    def load_grads(q, slot):
        return pltpu.make_async_copy(grads_all.at[pl.ds(2 * q, 2)], y_buf.at[slot], y_sem.at[slot])

    def load_own(buf, own, blocks, i):
        return [
            pltpu.make_async_copy(own, buf.at[0, k], own_sem.at[2 * i]),
            pltpu.make_async_copy(blocks.at[sibling], buf.at[0, 1 - k], own_sem.at[2 * i + 1]),
        ]

    def store_out(q, slot):
        return pltpu.make_async_copy(out_stage.at[slot], out_part.at[pl.ds(2 * q, 2)], o_sem.at[slot])

    def store_back(q, slot):
        return pltpu.make_async_copy(back_stage.at[slot], back_part.at[pl.ds(2 * q, 2)], b_sem.at[slot])

    @pl.when(p < line - 1)
    def _():
        along(p, hidden, True).start()

    @pl.when(p > 0)
    def _():
        along(p, hidden, False).start()

    across(p, hidden).start()
    if hop:
        hops = Gathering(line, grads_all.at[e], grads_all, refs[31:36], window=(rows // 2, rows // 2))
        hops.forward(2)
    for copy in load_own(y_buf, own_grads, grads_all, 0):
        copy.start()

    def pump(d):
        for to_right in (True, False):
            q = p - d if to_right else p + d
            here = (q >= 0) if to_right else (q < line)
            further = (p < line - 1) if to_right else (p > 0)

            @pl.when(here)
            def _():
                block = hidden_all.at[2 * q + k]
                along(q, block, to_right).wait_recv()

                @pl.when(further)
                def _():
                    along(q, block, to_right).start()

                across(q, block).start()

    for copy in loads:
        copy.wait()

    lane = lax.broadcasted_iota(jnp.int32, (local * cap, lanes), 1)
    expert_of_row = lax.broadcasted_iota(jnp.int32, (local * cap, lanes), 0) // cap

    def units_of(j, q):
        tile = 256
        rows_j = xs[j].reshape(slots, width)
        xs_turned[j, :, pl.ds(pl.multiple_of(q * slots, slots), slots)] = rows_j.T
        grads_j = ds[j, q].reshape(slots, width)

        def units(t, carried):
            at = pl.ds(pl.multiple_of(t * tile, tile), tile)
            gate_pre = dot(rows_j, wg[j, :, at])
            up_pre = dot(rows_j, wu[j, :, at])
            grad_act = dot_nt(grads_j, wd[j, at, :])
            sigmoid = 1.0 / (1.0 + jnp.exp(-gate_pre))
            silu = gate_pre * sigmoid
            hidden_low = (silu * up_pre).astype(bf16)
            act[j, :, at] = hidden_low
            act_turned[j, at, pl.ds(pl.multiple_of(q * slots, slots), slots)] = hidden_low.T
            dg[j, q, :, at] = (grad_act * up_pre * sigmoid * (1.0 + gate_pre * (1.0 - sigmoid))).astype(bf16)
            du[j, q, :, at] = (grad_act * silu).astype(bf16)
            return carried

        lax.fori_loop(0, hidden_units // tile, units, 0)

    def give_back(q, slot):
        wide = 512
        pick_pair = [picks[b] for b in range(2)]

        def outputs(t, sums):
            at = pl.ds(pl.multiple_of(t * wide, wide), wide)
            gated, back, new_sums = [], [], []
            for j in range(local):
                y = dot(act[j], wd[j, :, at])
                back_j = dot_nt(dg[j, q], wg[j, at, :]) + dot_nt(du[j, q], wu[j, at, :])
                new = []
                for b in range(2):
                    half = slice(b * cap, (b + 1) * cap)
                    y_b = y[half]
                    new.append(sums[j][b] + jnp.sum(y_b * es[j, b, :, at].astype(f32), -1, keepdims=True))
                    gated.append((gate_kept[b, j * cap : (j + 1) * cap, 0:1] * y_b).astype(bf16))
                    back.append(back_j[half].astype(bf16))
                new_sums.append(tuple(new))
            for b in range(2):
                mine = jnp.concatenate([gated[2 * j + b] for j in range(local)], 0)
                out_stage[slot, b, :, at] = dot_tn(pick_pair[b], mine).astype(bf16)
                mine = jnp.concatenate([back[2 * j + b] for j in range(local)], 0)
                back_stage[slot, b, :, at] = dot_tn(pick_pair[b], mine).astype(bf16)
            return tuple(new_sums)

        nothing = jnp.zeros((cap, 1), f32)
        sums = lax.fori_loop(
            0, width // wide, outputs, tuple((nothing, nothing) for _ in range(local))
        )
        for b in range(2):
            grad_gates = jnp.concatenate([sums[j][b] for j in range(local)], 0)
            coarse = grad_gates.astype(bf16).astype(f32)
            spot = e * local + expert_of_row
            spread = jnp.where(
                lane == spot, coarse, jnp.where(lane == spot + lanes // 2, grad_gates - coarse, 0.0)
            ).astype(bf16)
            back_stage[slot, b, :, width : width + lanes] = dot_tn(pick_pair[b], spread).astype(bf16)
        store_out(q, slot).start()
        store_back(q, slot).start()

    def one_chip(i, carried):
        q, d, first = visit(p, line, i)
        slot = i % 2

        across(q, hidden).wait_recv()

        @pl.when(i == 0)
        def _():
            own = load_own(h_buf, hidden, hidden_all, 1)
            for copy in own:
                copy.start()
            for copy in own + load_own(y_buf, own_grads, grads_all, 0):
                copy.wait()

        @pl.when(i > 0)
        def _():
            load_hidden(q, slot).start()

        if hop:
            @pl.when(d == line - 1)
            def _():
                hops.pump(line - 1, onward=False)
                hops.finish([], [line - 1])
                load_grads(q, slot).start()

        after, d_after, _ = visit(p, line, i + 1)

        @pl.when((i < line - 1) & (d_after < (line - 1 if hop else line)))
        def _():
            load_grads(after, 1 - slot).start()

        @pl.when(i > 0)
        def _():
            load_hidden(q, slot).wait()
            load_grads(q, slot).wait()

        @pl.when(i >= 2)
        def _():
            store_out(visit(p, line, i - 2)[0], slot).wait()
            store_back(visit(p, line, i - 2)[0], slot).wait()

        place = lax.broadcasted_iota(jnp.int32, (cap, rows), 0).astype(f32)
        sub = lax.broadcasted_iota(jnp.int32, (lanes, rows), 0)
        upper = lax.broadcasted_iota(jnp.int32, (rows, 2 * rows), 0)
        column = lax.broadcasted_iota(jnp.int32, (rows, 2 * rows), 1)
        ahead = jnp.where((upper < column) & (column < rows) | (upper + rows == column), 1.0, 0.0).astype(bf16)
        for b in range(2):
            marks = named[2 * q + b]
            counted = dot_tn(marks, ahead)
            slots_of = jnp.where(counted[:, rows:] > 0.5, counted[:, :rows], -1.0)
            for j in range(local):
                row = jnp.sum(jnp.where(sub == e * local + j, slots_of, 0.0), 0, keepdims=True)
                picks[b, j * cap : (j + 1) * cap] = jnp.where(place == row, 1.0, 0.0).astype(bf16)
            pick = picks[b]
            block = h_buf[slot, b]
            picked = dot(pick, block).astype(bf16)
            for j in range(local):
                xs[j, b] = picked[j * cap : (j + 1) * cap]
            logits = jnp.where(marks.astype(f32) > 0.5, dot(block, router[...]), NEG)
            raised = jnp.exp(logits - jnp.max(logits, -1, keepdims=True))
            gates = raised / jnp.sum(raised, -1, keepdims=True)
            coarse = gates.astype(bf16)
            fine = (gates - coarse.astype(f32)).astype(bf16)
            at_slots = dot(pick, coarse) + dot(pick, fine)
            gate_slot = jnp.sum(jnp.where(lane == e * local + expert_of_row, at_slots, 0.0), -1, keepdims=True)
            gate_kept[b] = jnp.broadcast_to(gate_slot, gate_kept.shape[1:])
            grad_rows = dot(pick, y_buf[slot, b])
            grad_pairs = (gate_slot * grad_rows).astype(bf16)
            grad_rows = grad_rows.astype(bf16)
            for j in range(local):
                es[j, b] = grad_rows[j * cap : (j + 1) * cap]
                ds[j, q, b] = grad_pairs[j * cap : (j + 1) * cap]

        units_of(0, q)

        @pl.when(i < line - 1)
        def _():
            for j in range(1, local):
                units_of(j, q)
            give_back(q, slot)

        @pl.when(first & (d + 1 < line))
        def _():
            pump(d + 1)

        return carried

    lax.fori_loop(0, line, one_chip, 0)

    deep = line * slots
    tile = 256
    tiles = hidden_units // tile

    def products(left, right, stage, first_row, count):
        high = stage.shape[1]

        def stores(t):
            row = first_row + lax.div(t, tiles) * high
            return pltpu.make_async_copy(
                stage.at[lax.rem(t, 2)],
                grads.at[
                    pl.ds(pl.multiple_of(row, 16), high),
                    pl.ds(pl.multiple_of(lax.rem(t, tiles) * tile, tile), tile),
                ],
                s_sem.at[lax.rem(t, 2)],
            )

        def one_tile(t, carried):
            @pl.when(t >= 2)
            def _():
                stores(t - 2).wait()

            stage[lax.rem(t, 2)] = dot(left[...], right(pl.ds(pl.multiple_of(t * tile, tile), tile))).astype(bf16)
            stores(t).start()
            return carried

        lax.fori_loop(0, count, one_tile, 0)
        for t in range(max(0, count - 2), count):
            stores(jnp.int32(t)).wait()

    totals = Totals(grads, early_first, *refs[-2:]) if start else None
    sent = 0

    def send_ready(rows_done):
        nonlocal sent
        while start and sent < totals.early and (sent + 1) * totals.deep <= rows_done:
            totals.start_early(sent)
            sent += 1

    last_chip = visit(p, line, jnp.int32(line - 1))[0]
    for i, source in enumerate((dg, du)):
        for j in range(local):
            if i == 0 and j > 0:
                units_of(j, last_chip)
            products(
                xs_turned.at[j],
                lambda at: source[j, :, :, at].reshape(deep, tile),
                in_stage, (i * local + j) * width, tiles,
            )
            send_ready((i * local + j + 1) * width)
    for j in range(local):
        products(
            act_turned.at[j],
            lambda at: ds[j, :, :, :, at].reshape(deep, tile),
            down_stage, 2 * local * width + j * width, width // tile,
        )

    give_back(last_chip, (line - 1) % 2)

    if start:
        totals.end_early()
    if hop:
        hops.finish([2], [])
    for i in range(max(0, line - 2), line):
        q = visit(p, line, jnp.int32(i))[0]
        store_out(q, i % 2).wait()
        store_back(q, i % 2).wait()
    for d in range(line):
        for to_right in (True, False):
            if d == 0 and not to_right:
                continue
            q = p - d if to_right else p + d
            here = (q >= 0) if to_right else (q < line)

            @pl.when(here)
            def _():
                across(q, hidden).wait_send()
    for d in range(line):
        for to_right in (True, False):
            q = p - d if to_right else p + d
            here = (q >= 0) if to_right else (q < line)
            further = (p < line - 1) if to_right else (p > 0)

            @pl.when(here & further)
            def _():
                along(q, hidden, to_right).wait_send()


def expert_pass(hop, start, cap, hidden, own_grads, grads_all, named, router, w_gate, w_up, w_down, collective_id):
    n = lax.axis_size("exp")
    line = n // 2
    rows, width = hidden.shape
    local, _, units = w_gate.shape
    bf16 = jnp.bfloat16
    lanes = router.shape[1]
    dma = pltpu.SemaphoreType.DMA
    vmem = pl.BlockSpec(memory_space=pltpu.VMEM)
    slots = n * cap
    return pl.pallas_call(
        functools.partial(expert_kernel, line, local, cap, hop, start),
        out_shape=(
            jax.ShapeDtypeStruct((n, rows, width), bf16),
            jax.ShapeDtypeStruct((n, rows, width), bf16),
            jax.ShapeDtypeStruct((n, rows, width + lanes), bf16),
            jax.ShapeDtypeStruct((3 * local * width, units), bf16),
            jax.ShapeDtypeStruct(grads_all.shape, bf16),
        )
        + ((Totals.early_landing(3 * local * width // Totals.count, units),) if start else ()),
        in_specs=[ANY, ANY, ANY, vmem, vmem, ANY, ANY, ANY],
        out_specs=(ANY,) * (6 if start else 5),
        input_output_aliases={2: 4},
        scratch_shapes=[
            pltpu.VMEM((local, width, units), bf16),
            pltpu.VMEM((local, width, units), bf16),
            pltpu.VMEM((local, units, width), bf16),
            pltpu.VMEM((local, 2, cap, width), bf16),
            pltpu.VMEM((local, line, 2, cap, width), bf16),
            pltpu.VMEM((local, 2 * cap, units), bf16),
            pltpu.VMEM((local, line, 2 * cap, units), bf16),
            pltpu.VMEM((local, line, 2 * cap, units), bf16),
            pltpu.VMEM((local, 2, cap, width), bf16),
            pltpu.VMEM((2, 2, rows, width), bf16),
            pltpu.VMEM((2, 2, rows, width), bf16),
            pltpu.VMEM((2, 2, rows, width), bf16),
            pltpu.VMEM((2, 2, rows, width + lanes), bf16),
            pltpu.VMEM((2, width, 256), bf16),
            pltpu.VMEM((2, units, 256), bf16),
            pltpu.VMEM((2, local * cap, rows), bf16),
            pltpu.VMEM((local, width, n * cap), bf16),
            pltpu.VMEM((local, units, n * cap), bf16),
            pltpu.VMEM((2, local * cap, 128), jnp.float32),
            dma((3,)),
            dma((4,)),
            dma((2, line)),
            dma((line,)),
            dma((line,)),
            dma((line,)),
            dma((2,)),
            dma((2,)),
            dma((2,)),
            dma((2,)),
            dma((2,)),
        ]
        + (Gathering.scratch(line) if hop else [])
        + (Totals.early_scratch() if start else []),
        compiler_params=pltpu.CompilerParams(
            collective_id=collective_id, has_side_effects=True, vmem_limit_bytes=62 << 20
        ),
        name="expert_pass",
    )(hidden, own_grads, grads_all, named, router, w_gate, w_up, w_down)


def turn(block, cosine, signed_sine):
    return block * cosine + pltpu.roll(block, block.shape[1] // 2, 1) * signed_sine


def row_norm(block):
    inverse = lax.rsqrt(jnp.mean(block * block, -1, keepdims=True) + EPS)
    return block * inverse, inverse


def attend_kernel(size, line, hop, experts, heads, kv_heads, tokens, small, cosine, sine, qkv_hbm, out_hbm, rows_in, *refs):
    targets, rows_all = refs[:7], refs[7]
    held, refs = refs[8:15], refs[15:]
    queries, keyval, mixed, lse, mid, hidden, gains = held
    wqkv, wout, h1, w_sem, send, recv, o_sem = refs[:7]
    f32, bf16 = jnp.float32, jnp.bfloat16
    c, e = lax.axis_index("ctx"), lax.axis_index("exp")
    rows, width = tokens.shape
    head = HEAD_WIDTH
    groups = heads // kv_heads
    q_width, kv_width = heads * head, kv_heads * head
    loads = [
        pltpu.make_async_copy(qkv_hbm, wqkv, w_sem.at[0]),
        pltpu.make_async_copy(out_hbm, wout, w_sem.at[1]),
    ]
    for copy in loads:
        copy.start()
    others = [lax.rem(c + i, size) for i in range(1, size)]
    column = [(e >= 2, c, e - 2), (e < 2 * line - 2, c, e + 2), (True, c, e + 1 - 2 * (e % 2))]
    greet((column if hop else []) + [(True, there, e) for there in others])
    if hop:
        half = rows // 2
        early, late = (
            Gathering(line, rows_all.at[e], rows_all, refs[7 + 5 * i : 12 + 5 * i], window=(i * half, half)) for i in range(2)
        )
        early.forward(1)
        late.forward(1)

    def leave(i):
        return pltpu.make_async_copy(held[i], targets[i], o_sem.at[i])

    turned = small[...].astype(f32).T
    gains[...] = turned[experts : experts + 8]
    leave(6).start()

    def step(t, carried):
        at = pl.ds(pl.multiple_of(t * 64, 64), 64)
        normed, _ = row_norm(tokens[at, :].astype(f32))
        h1[at, :] = (normed * gains[0:1, :]).astype(bf16)
        return carried

    lax.fori_loop(0, rows // 64, step, 0)
    loads[0].wait()
    kv = dot(h1[...], wqkv[:, q_width:])
    for j in range(kv_heads):
        at = slice(j * head, (j + 1) * head)
        keyval[c, :, at] = turn(kv[:, at], cosine[...], sine[...]).astype(bf16)
    keyval[c, :, kv_width:] = kv[:, kv_width:].astype(bf16)

    def give(i):
        return remote(keyval.at[c], keyval.at[c], send.at[i - 1], recv.at[i - 1], others[i - 1], e)

    for i in range(1, size):
        @pl.when(c + i < size)
        def _():
            give(i).start()

    for j in range(1, size):
        @pl.when(j > c)
        def _():
            keyval[j] = jnp.zeros((rows, 2 * kv_width), bf16)

    pair = 2 * head

    def project(t, carried):
        at = pl.ds(pl.multiple_of(t * pair, pair), pair)
        q = dot(h1[...], wqkv[:, at])
        for j in range(2):
            queries[2 * t + j] = turn(q[:, j * head : (j + 1) * head], cosine[...], sine[...]).astype(bf16)
        return carried

    lax.fori_loop(0, heads // 2, project, 0)
    leave(0).start()
    if hop:
        early.pump(2)
    for i in range(1, size):
        @pl.when(c - i >= 0)
        def _():
            give(i).wait_recv()
    leave(1).start()

    keys_count = size * rows
    scaling = 1.0 / math.sqrt(head)
    lane = lax.broadcasted_iota(jnp.int32, (rows, 128), 1)

    def one_head(j):
        h = j // groups
        keys = keyval[:, :, pl.ds(pl.multiple_of(h * head, head), head)].reshape(keys_count, head)
        values = keyval[:, :, pl.ds(pl.multiple_of(kv_width + h * head, head), head)].reshape(keys_count, head)
        place = lax.broadcasted_iota(jnp.int32, (rows, keys_count), 1)
        row = c * rows + lax.broadcasted_iota(jnp.int32, (rows, keys_count), 0)
        scores = jnp.where(place <= row, dot_nt(queries[j], keys) * scaling, NEG)
        peak = jnp.max(scores, -1, keepdims=True)
        raised = jnp.exp(scores - peak)
        total = jnp.sum(raised, -1, keepdims=True)
        probs = (raised * (1.0 / total)).astype(bf16)
        return dot(probs, values), peak + jnp.log(total)

    def two_heads(t, stats):
        found = [one_head(2 * t + i) for i in range(2)]
        mixed[:, pl.ds(pl.multiple_of(t * pair, pair), pair)] = jnp.concatenate(
            [block for block, _ in found], 1
        ).astype(bf16)
        for i, (_, value) in enumerate(found):
            stats = jnp.where(lane == 2 * t + i, value, stats)
        return stats

    lse[...] = lax.fori_loop(0, heads // 2, two_heads, jnp.zeros((rows, 128), f32))
    leave(2).start()
    leave(3).start()
    if hop:
        late.pump(2, onward=False)
    loads[1].wait()

    def outward(t, carried):
        at = pl.ds(pl.multiple_of(t * 256, 256), 256)
        mid[:, at] = tokens[:, at].astype(f32) + dot(mixed[...], wout[:, at])
        return carried

    lax.fori_loop(0, width // 256, outward, 0)
    leave(4).start()

    def last(t, carried):
        at = pl.ds(pl.multiple_of(t * 64, 64), 64)
        normed, _ = row_norm(mid[at, :])
        hidden[at, :] = (normed * gains[1:2, :]).astype(bf16)
        return carried

    lax.fori_loop(0, rows // 64, last, 0)
    leave(5).start()
    if hop:
        early.pump(3, onward=False)
        early.finish([1, 2], [2, 3])
        late.finish([1], [2])
    for i in range(7):
        leave(i).wait()
    for i in range(1, size):
        @pl.when(c + i < size)
        def _():
            give(i).wait_send()


def attend(hop, experts, tokens, small, cosine, sine, qkv_full, out_full, rows_all, collective_id):
    size, line = lax.axis_size("ctx"), lax.axis_size("exp") // 2
    rows, width = tokens.shape
    f32, bf16 = jnp.float32, jnp.bfloat16
    dma = pltpu.SemaphoreType.DMA
    vmem = pl.BlockSpec(memory_space=pltpu.VMEM)
    shape = jax.ShapeDtypeStruct
    made = (
        shape((QUERY_HEADS, rows, HEAD_WIDTH), bf16),
        shape((size, rows, 2 * KEY_VALUE_HEADS * HEAD_WIDTH), bf16),
        shape((rows, QUERY_HEADS * HEAD_WIDTH), bf16),
        shape((rows, 128), f32),
        shape((rows, width), f32),
        shape((rows, width), bf16),
        shape((8, width), f32),
    )
    return pl.pallas_call(
        functools.partial(attend_kernel, size, line, hop, experts, QUERY_HEADS, KEY_VALUE_HEADS),
        out_shape=made + (shape(rows_all.shape, bf16),),
        in_specs=[vmem] * 4 + [ANY] * 3,
        out_specs=(ANY,) * 8,
        input_output_aliases={6: 7},
        scratch_shapes=[pltpu.VMEM(one.shape, one.dtype) for one in made]
        + [
            pltpu.VMEM(qkv_full.shape, bf16),
            pltpu.VMEM(out_full.shape, bf16),
            pltpu.VMEM((rows, width), bf16),
            dma((2,)),
            dma((size - 1,)),
            dma((size - 1,)),
            dma((7,)),
        ]
        + (Gathering.scratch(line) * 2 if hop else []),
        compiler_params=pltpu.CompilerParams(
            collective_id=collective_id, has_side_effects=True, vmem_limit_bytes=62 << 20
        ),
        name="attend",
    )(tokens, small, cosine, sine, qkv_full, out_full, rows_all)


def halves(values):
    coarse = values.astype(jnp.bfloat16)
    return coarse, (values - coarse.astype(jnp.float32)).astype(jnp.bfloat16)


def backward_kernel(size, line, heads, kv_heads, experts, fused, *refs):
    back_part, out_part, grads, early_first, tokens, mid, final, marks, small, gains = refs[:10]
    queries, keyval, mixed, lse, cosine, sine, qkv_hbm, out_hbm, output, grad_tokens, dense_out, dense_qkv = refs[10:22]
    refs = refs[22:]
    if fused:
        totals, total_out, total_qkv, land_one, land_two = refs[:5]
        landing, refs = refs[5:13], refs[13:]
        tmp = refs[0]
        sum_refs, refs = [refs[1 + 7 * i : 8 + 7 * i] for i in range(4)], refs[29:]
        total_scratch, refs = refs[:8], refs[8:]
        share_out, share_qkv, refs = refs[:7], refs[7:14], refs[14:]
    else:
        came, out_sum = back_part, out_part
    wqkv, wout, probs, d_scores, d_mixed, d_att, d_mid, h1, h2, dq, dkv, kv_part, kv_other, stage = refs[:14]
    w_sem, kv_send, kv_recv, s_sem = refs[14:]
    f32, bf16 = jnp.float32, jnp.bfloat16
    c, e = lax.axis_index("ctx"), lax.axis_index("exp")
    p, k = e // 2, e % 2
    rows, width = tokens.shape
    head = HEAD_WIDTH
    groups = heads // kv_heads
    q_width, kv_width = heads * head, kv_heads * head
    scaling = 1.0 / math.sqrt(head)
    keys_count = size * rows
    n = 2 * line
    shard = dense_out.shape[1]

    loads = [
        pltpu.make_async_copy(qkv_hbm, wqkv, w_sem.at[0]),
        pltpu.make_async_copy(out_hbm, wout, w_sem.at[1]),
    ]
    others = [lax.rem(c + i, size) for i in range(1, size)]
    column = [(p > 0, c, e - 2), (p < line - 1, c, e + 2), (True, c, e + 1 - 2 * k)]
    greet((column if fused else []) + [(True, there, e) for there in others])
    ticked = []

    def tick():
        if fused and len(ticked) < experts_total.ticks:
            experts_total.tick(len(ticked))
            ticked.append(1)

    if fused:
        experts_total = Totals(
            grads, early_first, *total_scratch[3:5], totals, land_one, land_two, total_scratch[:3], total_scratch[5:]
        )
        experts_total.begin()
        sums = [
            Summing(line, part, landing[2 * i], landing[2 * i + 1], sum_refs[i][0], tmp, sum_refs[i][1:])
            for i, part in enumerate((back_part, out_part, dense_out, dense_qkv))
        ]
        back, outs, dense_outs, dense_qkvs = sums
        came, out_sum = back.result(), outs.result()
        sharing_out = Sharing(size, dense_outs.result(), total_out, *share_out[:2], share_out[2:])
        sharing_qkv = Sharing(size, dense_qkvs.result(), total_qkv, *share_qkv[:2], share_qkv[2:])
        back.begin()
    for copy in loads:
        copy.start()

    lane = lax.broadcasted_iota(jnp.int32, (rows, 128), 1)

    def keys_of(h):
        return keyval[:, :, pl.ds(pl.multiple_of(h * head, head), head)].reshape(keys_count, head)

    def values_of(h):
        return keyval[:, :, pl.ds(pl.multiple_of(kv_width + h * head, head), head)].reshape(keys_count, head)

    def again(j, carried):
        place = lax.broadcasted_iota(jnp.int32, (rows, keys_count), 1)
        row = c * rows + lax.broadcasted_iota(jnp.int32, (rows, keys_count), 0)
        scores = dot_nt(queries[j], keys_of(j // groups)) * scaling
        level = jnp.sum(jnp.where(lane == j, lse[...], 0.0), -1, keepdims=True)
        probs[j] = jnp.exp(jnp.where(place <= row, scores - level, NEG)).astype(bf16)
        return carried

    def norms(t, carried):
        at = pl.ds(pl.multiple_of(t * 64, 64), 64)
        normed, _ = row_norm(mid[at, :])
        h2[at, :] = (normed * gains[1:2, :]).astype(bf16)
        normed, _ = row_norm(tokens[at, :].astype(f32))
        h1[at, :] = (normed * gains[0:1, :]).astype(bf16)
        return carried

    bounds = [heads * i // max(1, line - 1) for i in range(line)]
    for i, d in enumerate(range(line - 1, 0, -1)):
        if fused and i > 0:
            back.step(d)
        if i == 0:
            lax.fori_loop(0, rows // 64, norms, 0)
        lax.fori_loop(bounds[i], bounds[i + 1], again, 0)
        tick()
        if fused and d == 2:
            outs.begin()
    if fused:
        back.step(0)
        tick()

    logits = jnp.where(marks[...].astype(f32) > 0.5, dot(h2[...], small[...]), NEG)
    raised = jnp.exp(logits - jnp.max(logits, -1, keepdims=True))
    gates = raised / jnp.sum(raised, -1, keepdims=True)
    extra = came[:, width:].astype(f32)
    grad_gates = extra + pltpu.roll(extra, extra.shape[1] // 2, 1)
    grad_logits = gates * (grad_gates - jnp.sum(gates * grad_gates, -1, keepdims=True))
    logits_hi, logits_lo = halves(grad_logits)
    grad_small = dot_tn(h2[...], logits_hi) + dot_tn(h2[...], logits_lo)

    def second_norm(t, total):
        at = pl.ds(pl.multiple_of(t * 32, 32), 32)
        normed, inverse = row_norm(mid[at, :])
        low, high = halves(grad_logits_ref[at, :])
        grad_h2 = came[at, :width].astype(f32) + dot_nt(low, small[...]) + dot_nt(high, small[...])
        total = total + jnp.sum(grad_h2 * normed, 0, keepdims=True)
        scaled = grad_h2 * gains[1:2, :]
        grad = final[at, :].astype(f32) + inverse * (scaled - normed * jnp.mean(scaled * normed, -1, keepdims=True))
        d_mid[at, :] = grad
        d_att[at, :] = grad.astype(bf16)
        return total

    grad_logits_ref = dkv.at[:, 0:128]
    dkv[:, 0:128] = grad_logits
    gain_two = lax.fori_loop(0, rows // 32, second_norm, jnp.zeros((1, width), f32))

    loads[1].wait()

    def mixing(t, carried):
        at = pl.ds(pl.multiple_of(t * 256, 256), 256)
        block = dot_nt(d_att[...], wout[at, :]).astype(bf16)
        for i in range(2):
            d_mixed[2 * t + i] = block[:, i * head : (i + 1) * head]
        return carried

    lax.fori_loop(0, q_width // 256, mixing, 0)
    if fused and line > 2:
        outs.step(line - 2)
    tick()

    def gradients(left, right, dense, column, count):
        def store(t):
            return pltpu.make_async_copy(
                stage.at[lax.rem(t, 2)],
                dense.at[:, :, pl.ds(pl.multiple_of(column + t * 256, 128), 256)],
                s_sem.at[lax.rem(t, 2)],
            )

        def one(t, carried):
            @pl.when(t >= 2)
            def _():
                store(t - 2).wait()

            product = dot_tn(left[...], right[:, pl.ds(pl.multiple_of(t * 256, 256), 256)])
            stage[lax.rem(t, 2)] = product.astype(bf16).reshape(n, shard, 256)
            store(t).start()
            return carried

        lax.fori_loop(0, count, one, 0)
        for t in range(max(0, count - 2), count):
            store(jnp.int32(t)).wait()

    gradients(mixed, d_att, dense_out, 0, width // 256)
    if fused:
        dense_outs.begin()
        tick()
        for d in range(line - 3, 0, -1):
            outs.step(d)

    def per_head(j, carried):
        grad_probs = dot_nt(d_mixed[j], values_of(j // groups))
        weights_now = probs[j].astype(f32)
        inner = jnp.sum(weights_now * grad_probs, -1, keepdims=True)
        grad = (weights_now * (grad_probs - inner) * scaling).astype(bf16)
        d_scores[lax.rem(j, groups)] = grad
        back_q = dot(grad, keys_of(j // groups))
        dq[:, pl.ds(pl.multiple_of(j * head, head), head)] = turn(back_q, cosine[...], -sine[...]).astype(bf16)
        return carried

    for h in range(kv_heads):
        lax.fori_loop(h * groups, (h + 1) * groups, per_head, 0)
        these = slice(h * groups, (h + 1) * groups)
        grad_keys = dot_tn(
            d_scores[...].reshape(groups * rows, keys_count), queries[these].reshape(groups * rows, head)
        )
        grad_values = dot_tn(
            probs[these].reshape(groups * rows, keys_count), d_mixed[these].reshape(groups * rows, head)
        )
        kv_part[:, :, h * head : (h + 1) * head] = grad_keys.astype(bf16).reshape(size, rows, head)
        at = kv_width + h * head
        kv_part[:, :, at : at + head] = grad_values.astype(bf16).reshape(size, rows, head)
        if h == 0 and fused:
            tick()
            outs.step(0)

    def give(i):
        there = lax.rem(c + size - i, size)
        return remote(kv_part.at[there], kv_other.at[i - 1], kv_send.at[i - 1], kv_recv.at[i - 1], there, e)

    for i in range(1, size):
        @pl.when(c - i >= 0)
        def _():
            give(i).start()

    tick()
    if fused and line > 2:
        dense_outs.step(line - 2)
    gradients(h1, dq, dense_qkv, 0, q_width // 256)
    tick()
    if fused:
        for d in range(line - 3, 0, -1):
            dense_outs.step(d)

    own = kv_part[c].astype(f32)
    dkv[...] = own
    for i in range(1, size):
        @pl.when(c + i < size)
        def _():
            give(i).wait_recv()
            dkv[...] += kv_other[i - 1].astype(f32)
    for j in range(kv_heads):
        at = slice(j * head, (j + 1) * head)
        dkv[:, at] = turn(dkv[:, at], cosine[...], -sine[...])
    dq[:, q_width:] = dkv[...].astype(bf16)
    dkv_low = dq.at[:, q_width:]
    gradients(h1, dkv_low, dense_qkv, q_width, 2 * kv_width // 256)
    loads[0].wait()

    def inputs(t, total):
        at = pl.ds(pl.multiple_of(t * 128, 128), 128)
        grad_h1 = dot_nt(dq[at, :], wqkv[...])
        normed, inverse = row_norm(tokens[at, :].astype(f32))
        total = total + jnp.sum(grad_h1 * normed, 0, keepdims=True)
        scaled = grad_h1 * gains[0:1, :]
        grad_tokens[at, :] = d_mid[at, :] + inverse * (
            scaled - normed * jnp.mean(scaled * normed, -1, keepdims=True)
        )
        return total

    gain_one = lax.fori_loop(0, rows // 128, inputs, jnp.zeros((1, width), f32))
    sub = lax.broadcasted_iota(jnp.int32, (128, width), 0)
    gain_rows = jnp.where(sub == experts, gain_one, jnp.where(sub == experts + 1, gain_two, 0.0))
    grad_small = (grad_small + gain_rows.T).astype(bf16).reshape(n, shard, 128)
    stage[0, :, :, 0:128] = grad_small
    small_store = pltpu.make_async_copy(
        stage.at[0, :, :, 0:128], dense_qkv.at[:, :, q_width + 2 * kv_width :], s_sem.at[0]
    )
    small_store.start()
    small_store.wait()
    tick()
    if fused:
        dense_qkvs.begin()

    def finish(t, carried):
        at = pl.ds(pl.multiple_of(t * 64, 64), 64)
        output[at, :] = (mid[at, :] + out_sum[at, :].astype(f32)).astype(bf16)
        return carried

    lax.fori_loop(0, rows // 64, finish, 0)
    if fused:
        tick()
        dense_outs.step(0)
        sharing_out.begin()
        for d in range(line - 2, -1, -1):
            tick()
            if d == 0:
                sharing_out.middle()
                tick()
            dense_qkvs.step(d)
        sharing_qkv.begin()
        tick()
        sharing_qkv.middle()
        while len(ticked) < experts_total.ticks:
            tick()
        for one in sums:
            one.end()
        sharing_out.end()
        sharing_qkv.end()
        experts_total.end()
    for i in range(1, size):
        @pl.when(c - i >= 0)
        def _():
            give(i).wait_send()


def backward(experts, shard, back_part, out_part, grads, early_first, tokens, mid, final, marks, small, gains, queries, keyval, mixed, lse,
             cosine, sine, qkv_full, out_full, collective_id):
    size, n = lax.axis_size("ctx"), lax.axis_size("exp")
    line = n // 2
    rows, width = tokens.shape
    heads, kv_heads, head = QUERY_HEADS, KEY_VALUE_HEADS, HEAD_WIDTH
    kv_both = 2 * kv_heads * head
    keys_count = size * rows
    f32, bf16 = jnp.float32, jnp.bfloat16
    dma = pltpu.SemaphoreType.DMA
    vmem = pl.BlockSpec(memory_space=pltpu.VMEM)
    shape = jax.ShapeDtypeStruct
    fused = planned(size, n, shard)
    out_width, qkv_width = width, qkv_full.shape[1] + small.shape[1]
    shapes = [
        shape((rows, width), bf16),
        shape((rows, width), f32),
        shape((n, shard, out_width), bf16),
        shape((n, shard, qkv_width), bf16),
    ]
    summing = []
    if fused:
        deep = grads.shape[0] // Totals.count
        shapes += [
            shape(grads.shape, bf16),
            shape((shard, out_width), bf16),
            shape((shard, qkv_width), bf16),
        ]
        shapes += Totals.landing(deep, grads.shape[1])
        for high, wide in ((rows, back_part.shape[2]), (rows, width), (shard, out_width), (shard, qkv_width)):
            shapes += Summing.landing(line, high, wide)
        widest = max(back_part.shape[2], width, out_width, qkv_width)
        summing = [
            pltpu.VMEM((2, rows, widest), bf16),
        ]
        for high, wide in ((rows, back_part.shape[2]), (rows, width), (shard, out_width), (shard, qkv_width)):
            summing += Summing.scratch(line, high, wide)
        summing += Totals.scratch(deep, grads.shape[1])
        summing += Sharing.scratch(size, shard, out_width) + Sharing.scratch(size, shard, qkv_width)
    else:
        back_part = lax.psum_scatter(back_part, "exp", scatter_dimension=0)
        out_part = lax.psum_scatter(out_part, "exp", scatter_dimension=0)
    found = pl.pallas_call(
        functools.partial(backward_kernel, size, line, heads, kv_heads, experts, fused),
        out_shape=tuple(shapes),
        in_specs=[ANY if fused else vmem] * 2 + [ANY] * 2 + [vmem] * 12 + [ANY] * 2,
        out_specs=(vmem, vmem) + (ANY,) * (len(shapes) - 2),
        scratch_shapes=summing
        + [
            pltpu.VMEM(qkv_full.shape, bf16),
            pltpu.VMEM(out_full.shape, bf16),
            pltpu.VMEM((heads, rows, keys_count), bf16),
            pltpu.VMEM((heads // kv_heads, rows, keys_count), bf16),
            pltpu.VMEM((heads, rows, head), bf16),
            pltpu.VMEM((rows, width), bf16),
            pltpu.VMEM((rows, width), f32),
            pltpu.VMEM((rows, width), bf16),
            pltpu.VMEM((rows, width), bf16),
            pltpu.VMEM((rows, heads * head + kv_both), bf16),
            pltpu.VMEM((rows, kv_both), f32),
            pltpu.VMEM((size, rows, kv_both), bf16),
            pltpu.VMEM((size - 1, rows, kv_both), bf16),
            pltpu.VMEM((2, n, shard, 256), bf16),
            dma((2,)),
            dma((size - 1,)),
            dma((size - 1,)),
            dma((2,)),
        ],
        compiler_params=pltpu.CompilerParams(
            collective_id=collective_id, has_side_effects=True, vmem_limit_bytes=62 << 20
        ),
        name="backward",
    )(back_part, out_part, grads, early_first, tokens, mid, final, marks, small, gains, queries, keyval, mixed, lse, cosine, sine,
      qkv_full, out_full)
    if fused:
        return found[:2] + found[4:7]
    dense_out, dense_qkv = (lax.psum_scatter(part, "exp", scatter_dimension=0) for part in found[2:4])
    return found[:2] + (lax.psum(grads, "ctx"), lax.psum(dense_out, "ctx"), lax.psum(dense_qkv, "ctx"))


def widen_kernel(total, dense_out, dense_qkv, gate, up, down, w_out, w_query, w_keyval, held, held_out, held_qkv, *refs):
    wide, wide_out, wide_query, wide_keyval, in_sem, out_sem, dense_in, dense_done = refs
    f32 = jnp.float32
    high = held.shape[1]
    blocks, slots = held.shape[0], wide.shape[0]
    per, tall = blocks // 3, gate.shape[1] // high

    def load(i):
        return pltpu.make_async_copy(total.at[pl.ds(i * high, high)], held.at[i], in_sem.at[i])

    def store(i):
        n, at = i // per, i % per
        if n < 2:
            target = (gate, up)[n].at[at // tall, pl.ds(at % tall * high, high)]
        else:
            target = down.at[at // tall, :, pl.ds(at % tall * high, high)]
        return pltpu.make_async_copy(wide.at[i % slots], target, out_sem.at[i % slots])

    small_in = [
        pltpu.make_async_copy(src, dst, dense_in.at[i])
        for i, (src, dst) in enumerate(((dense_out, held_out), (dense_qkv, held_qkv)))
    ]
    small_done = [
        pltpu.make_async_copy(src, dst, dense_done.at[i])
        for i, (src, dst) in enumerate(((wide_out, w_out), (wide_query, w_query), (wide_keyval, w_keyval)))
    ]
    load(0).start()
    for copy in small_in:
        copy.start()
    for i in range(1, blocks):
        load(i).start()
    for i in range(blocks):
        load(i).wait()
        if i >= slots:
            store(i - slots).wait()
        wide[i % slots] = held[i].astype(f32)
        store(i).start()
        if i == 0:
            for copy in small_in:
                copy.wait()
            split = w_query.shape[1]
            wide_out[...] = held_out[...].astype(f32)
            wide_query[...] = held_qkv[:, :split].astype(f32)
            wide_keyval[...] = held_qkv[:, split : split + w_keyval.shape[1]].astype(f32)
            for copy in small_done:
                copy.start()
    for i in range(max(0, blocks - slots), blocks):
        store(i).wait()
    for copy in small_done:
        copy.wait()


def widen(total, dense_out, dense_qkv, local, width, units, q_width, kv_both):
    f32 = jnp.float32
    blocks, slots = total.shape[0] // units, 4
    shard = dense_out.shape[0]
    shape = jax.ShapeDtypeStruct
    dma = pltpu.SemaphoreType.DMA
    dense = [(shard, width), (shard, q_width), (shard, kv_both)]
    return pl.pallas_call(
        widen_kernel,
        out_shape=(
            shape((local, width, units), f32),
            shape((local, width, units), f32),
            shape((local, units, width), f32),
            *(shape(one, f32) for one in dense),
        ),
        in_specs=[ANY] * 3,
        out_specs=(ANY,) * 6,
        scratch_shapes=[
            pltpu.VMEM((blocks, units, units), total.dtype),
            pltpu.VMEM(dense_out.shape, dense_out.dtype),
            pltpu.VMEM(dense_qkv.shape, dense_qkv.dtype),
            pltpu.VMEM((slots, units, units), f32),
            *(pltpu.VMEM(one, f32) for one in dense),
            dma((blocks,)),
            dma((slots,)),
            dma((2,)),
            dma((3,)),
        ],
        compiler_params=pltpu.CompilerParams(vmem_limit_bytes=56 << 20),
        name="widen",
    )(total, dense_out, dense_qkv)


def rope_tables(first_row, row_count, head_size):
    half_size = head_size // 2
    frequency = ROPE_BASE ** (-jnp.arange(half_size, dtype=jnp.float32) * (2.0 / head_size))
    places = (first_row + jnp.arange(row_count, dtype=jnp.int32)).astype(jnp.float32)
    angles = places[:, None] * frequency[None, :]
    cosine = jnp.cos(angles)
    sine = jnp.sin(angles)
    return (jnp.concatenate([cosine, cosine], 1), jnp.concatenate([-sine, sine], 1))


def ein(spec, a, b):
    return jnp.einsum(spec, a, b, preferred_element_type=jnp.float32)


def shards(
    tokens,
    routes,
    gain_attn,
    w_query,
    key_value_weight,
    w_out,
    gain_ffn,
    w_router,
    w_gate,
    w_up,
    w_down,
    cotangent,
):
    f32 = jnp.float32
    bf16 = jnp.bfloat16
    rows, width = tokens.shape[1:]
    ctx_size, exp_size = lax.axis_size("ctx"), lax.axis_size("exp")
    ctx_index, exp_index = lax.axis_index("ctx"), lax.axis_index("exp")
    local_experts = w_gate.shape[0]
    experts = local_experts * exp_size
    top = routes.shape[2]
    capacity = 2 * rows * top // experts
    shard_rows = w_query.shape[0]
    heads, kv_heads, head = QUERY_HEADS, KEY_VALUE_HEADS, HEAD_WIDTH
    groups = heads // kv_heads
    q_width, kv_width = heads * head, kv_heads * head
    scaling = 1.0 / math.sqrt(head)
    first_row = ctx_index * rows

    named_own = jnp.any(routes[0][:, :, None] == jnp.arange(128, dtype=jnp.int32), axis=1).astype(bf16)
    small = jnp.concatenate(
        [
            w_router,
            gain_attn[:, None],
            gain_ffn[:, None],
            jnp.zeros((shard_rows, 128 - experts - 2), bf16),
        ],
        1,
    )
    qkv_full, out_full, small_full, named, rows_all = gather_weights(
        (jnp.concatenate([w_query, key_value_weight], 1), w_out, small), named_own, cotangent[0], 1
    )

    cosine, sine = rope_tables(first_row, rows, head)
    hops = planned(ctx_size, exp_size, shard_rows)
    queries, keyval, mixed, lse, resid_mid, hidden_two, gains, rows_all = attend(
        hops, experts, tokens[0], small_full, cosine, sine, qkv_full, out_full, rows_all, 2
    )

    _, out_part, back_part, grads, *early_first = expert_pass(
        hops and exp_size > 6, hops, capacity, hidden_two, cotangent[0], rows_all, named, small_full, w_gate, w_up, w_down, 3
    )
    output, grad_input, grads, dense_out, dense_qkv = backward(
        experts, shard_rows, back_part, out_part, grads, early_first[-1], tokens[0], resid_mid, cotangent[0], named_own, small_full, gains,
        queries, keyval, mixed, lse, cosine, sine, qkv_full, out_full, 4
    )
    small_total = dense_qkv[:, q_width + 2 * kv_width :].astype(f32)
    grad_gate, grad_up, grad_down, grad_out, grad_query, grad_keyval = widen(
        grads, dense_out, dense_qkv, local_experts, width, w_gate.shape[2], q_width, 2 * kv_width
    )
    return (
        output[None],
        grad_input[None],
        small_total[:, experts],
        grad_query,
        grad_keyval,
        grad_out,
        small_total[:, experts + 1],
        small_total[:, :experts],
        grad_gate,
        grad_up,
        grad_down,
    )


def solution(mesh):
    rows, wide, deep = P("exp", "ctx", None), P("exp", None), P("exp", None, None)
    flat = P("exp")
    return jax.shard_map(
        shards,
        mesh=mesh,
        in_specs=(rows, rows, flat, wide, wide, wide, flat, wide, deep, deep, deep, rows),
        out_specs=(rows, rows, flat, wide, wide, wide, flat, wide, deep, deep, deep),
        check_vma=False,
    )
```

profile of v0, /device:TPU:0, one launch (start us, length us, event | category | flops | bytes accessed | tf_op | source)
XLA Modules:
  0.0 488.7 jit_solution(7323657993331660789)
XLA Ops:
  0.7 0.1 pad.7.clone
  0.7 0.9 fusion
  1.7 0.6 convert_element_type.13.refs_3_.refs_7_
  2.3 0.7 broadcast_in_dim.23
  3.1 0.7 broadcast_in_dim.24
  3.8 0.8 copy.33
  4.6 0.7 maximum_maximum_fusion.refs_2_
  5.3 0.5 fusion.1
  5.9 0.8 pad_maximum_fusion.1
  6.7 2.1 pad_maximum_fusion.refs_0_
  8.9 54.8 %gather_weights.1 = (bf16[1536,2048]{1,0:T(8,128)(2,1)}, bf16[1536,1536]{1,0:T(8,128)(2,1)}, bf16[1536,128]{1,0:T(8,128)(2,1)}, bf16[8,256,128]{2,1,0:T(8,128)(2,1)}, bf16[8,256,1536]{2,1,0:T(8,128)(2,1)}) custom-call(bf16[192,2048]{1,0:T(8,128)(2,1)} %pad_maximum_fusion.refs_0_, bf16[192,1536]{1,0:T(8,128)(2,1)} %refs_1_.1, ...), custom_call_target="tpu_custom_call" | custom-call | tf_op jit(solution)/shard_map/gather_weights/pallas_call | solution.py:676
  63.7 35.2 %attend.1 = (bf16[12,256,128]{2,1,0:T(8,128)(2,1)}, bf16[4,256,512]{2,1,0:T(8,128)(2,1)}, bf16[256,1536]{1,0:T(8,128)(2,1)}, f32[256,128]{1,0:T(8,128)}, f32[256...) custom-call(bf16[256,1536]{1,0:T(8,128)(2,1)} %bitcast.9, ...), custom_call_target="tpu_custom_call", output_to_operand_aliasing={{7}: (6, {})} | custom-call | tf_op jit(solution)/shard_map/attend/pallas_call | solution.py:1284
  98.8 111.0 %expert_pass.1 = (bf16[8,256,1536]{2,1,0:T(8,128)(2,1)}, bf16[8,256,1536]{2,1,0:T(8,128)(2,1)}, bf16[8,256,1664]{2,1,0:T(8,128)(2,1)}, bf16[9216,768]{1,0:T(8,12...) custom-call(bf16[256,1536]{1,0:T(8,128)(2,1)} %get-tuple-element.43.hidd, ...), custom_call_target="tpu_custom_call", output_to_operand_aliasing={{4}: (2, {})} | custom-call | tf_op jit(solution)/shard_map/expert_pass/pallas_call | solution.py:1063
  209.8 258.2 %backward.1 = (bf16[256,1536]{1,0:T(8,128)(2,1)}, f32[256,1536]{1,0:T(8,128)}, bf16[8,192,1536]{2,1,0:T(8,128)(2,1)}, bf16[8,192,2176]{2,1,0:T(8,128)(2,1)}, bf1...) custom-call(bf16[8,256,1664]{2,1,0:T(8,128)(2,1)} %get-tuple-element, ...), custom_call_target="tpu_custom_call" | custom-call | tf_op jit(solution)/shard_map/backward/pallas_call | solution.py:1635
  468.1 0.8 slice_convert_fusion
  468.9 0.8 slice_reduce_fusion
  469.7 0.7 copy.36
  470.4 0.0 copy-start.1
  470.4 0.0 copy-start
  470.4 15.8 %widen.1 = (f32[2,1536,768]{2,1,0:T(8,128)}, f32[2,1536,768]{2,1,0:T(8,128)}, f32[2,768,1536]{2,1,0:T(8,128)}, f32[192,1536]{1,0:T(8,128)}, f32[192,1536]{1,0:T(8,128)}, /*index=5*/f32[192,512]{1,0:T(8,128)}) custom-call(bf16[9216,768]{1,0:T(8,128)(2,1)} %get-tuple-element.59.total, bf16[192,1536]{1,0:T(8,128)(2,1)} %get-tuple-element.60.dense_out, ...), custom_call_target="tpu_custom_call" | custom-call | tf_op jit(solution)/shard_map/widen/pallas_call | solution.py:1732
  486.2 0.0 copy-done.1
  486.2 0.9 copy.41
  487.1 0.0 copy-done
  487.1 1.1 copy.42
  (3 shorter events, 0.0 us)
Async XLA Ops:
  470.4 15.8 %copy-start.1 = (bf16[256,1536]{1,0:T(8,128)(2,1)S(1)}, bf16[256,1536]{1,0:T(8,128)(2,1)}, u32[]{:S(2)}) copy-start(bf16[256,1536]{1,0:T(8,128)(2,1)} %get-tuple-element.56) | copy-start | bytes 2359300
  470.4 16.7 %copy-start = (f32[256,1536]{1,0:T(8,128)S(1)}, f32[256,1536]{1,0:T(8,128)}, u32[]{:S(2)}) copy-start(f32[256,1536]{1,0:T(8,128)} %get-tuple-element.57) | copy-start | bytes 4718596
where the time goes:
time: 496 us; the launch traced here: 489 us
  Pallas kernels  475 us (96%)
  other arithmetic  6.61 us (1%)
  local copies, waits for them, and re-layouts  5.89 us (1%)
    pallas_call x1, Pallas kernels, backward(): pl.pallas_call(functools.partial(backward_kernel, size, line, heads, kv_h...  258 us
    pallas_call x1, Pallas kernels, expert_pass(): pl.pallas_call(functools.partial(expert_kernel, line, local, cap, hop, st...  111 us
    pallas_call x1, Pallas kernels, gather_weights(): pl.pallas_call(functools.partial(weights_kernel, line, shards[0].shape[0]...  54.8 us
    pallas_call x1, Pallas kernels, attend(): pl.pallas_call(functools.partial(attend_kernel, size, line, hop, experts,...  35.2 us
    pallas_call x1, Pallas kernels, widen(): pl.pallas_call(widen_kernel, out_shape=(shape((local, width, units), f32)...  15.8 us

commit v1 on v0

--- a/solution.py
+++ b/solution.py
@@ -161,8 +161,8 @@
 
 
 class Summing:
-    def __init__(self, line, part, cross, moving, acc, tmp, sems):
-        self.line, self.part, self.cross, self.moving = line, part, cross, moving
+    def __init__(self, line, part, cross, moving, acc, tmp, sems, early=None):
+        self.line, self.part, self.cross, self.moving, self.early = line, part, cross, moving, early
         self.acc, self.tmp = acc, tmp
         self.own_sem, self.tmp_sem, self.c_send, self.c_recv, self.z_send, self.z_recv = sems
         self.c, self.e = lax.axis_index("ctx"), lax.axis_index("exp")
@@ -198,7 +198,10 @@
             if d > 0 or to_right:
                 q = self.p + d if to_right else self.p - d
                 here = (q < self.line) if to_right else (q >= 0)
-                yield to_right, q, here, ((self.p > 0) if to_right else (self.p < self.line - 1))
+                behind = (self.p > 0) if to_right else (self.p < self.line - 1)
+                if d == 1 and self.early is not None:
+                    here = here & behind
+                yield to_right, q, here, behind
 
     def begin(self):
         order = [(d, end) for d in range(self.line - 1, -1, -1) for end in self.ends(d)]
@@ -239,7 +242,18 @@
             return
         last = ((0, self.p, self.p > 0), (1, self.line, self.p < self.line - 1))
         for side, place, behind in last:
-            @pl.when(behind)
+            if self.early is not None:
+                from_end = (self.p == 1) if side == 0 else (self.p == self.line - 2)
+
+                @pl.when(from_end)
+                def _():
+                    self.load(self.early, side).start()
+
+                arrives = behind & jnp.logical_not(from_end)
+            else:
+                arrives = behind
+
+            @pl.when(arrives)
             def _():
                 self.arrived(place).wait_recv()
                 self.load(self.moving.at[place], side).start()
@@ -447,73 +461,88 @@
 
 
 class Sharing:
-    def __init__(self, size, part, total, summed, arrived, sems):
-        self.size, self.part, self.total, self.summed, self.arrived_at = size, part, total, summed, arrived
-        self.a_send, self.a_recv, self.b_send, self.b_recv, self.store_sem = sems
-        self.c, self.e = lax.axis_index("ctx"), lax.axis_index("exp")
-        self.piece = part.shape[0] // size
-
-    def rows(self, ref, j):
-        return ref.at[pl.ds(pl.multiple_of(j * self.piece, 16), self.piece), :]
-
-    def there(self, i):
-        return lax.rem(self.c + i + 1, self.size)
-
-    def give(self, i):
-        there = self.there(i)
-        return remote(
-            self.rows(self.part, there), self.arrived_at.at[i], self.a_send.at[i], self.a_recv.at[i], there, self.e
+    def __init__(self, part, total, landed, sems):
+        self.part, self.total = part, total
+        self.one, self.two = landed[:2], landed[2:]
+        self.sends, self.recvs, self.store_sem = sems
+        c, self.e = lax.axis_index("ctx"), lax.axis_index("exp")
+        self.bits = (c % 2, c // 2)
+        self.nbrs = (c + 1 - 2 * (c % 2), lax.rem(c + 2, 4))
+        self.rows, self.width = part.shape
+
+    @staticmethod
+    def columns(width):
+        first = width // 256 * 128
+        return ((0, first), (first, width - first))
+
+    def window(self, ref, h, kept_one, kept_two=None):
+        one, two = (0, 1) if h == 0 else (1, 0)
+        half, quarter = self.rows // 2, self.rows // 4
+        start = (self.bits[one] if kept_one else 1 - self.bits[one]) * half
+        count = half
+        if kept_two is not None:
+            start = start + (self.bits[two] if kept_two else 1 - self.bits[two]) * quarter
+            count = quarter
+        return ref.at[pl.ds(pl.multiple_of(start, 16), count), pl.ds(*self.columns(self.width)[h])]
+
+    def copy(self, stage, h):
+        one, two = (0, 1) if h == 0 else (1, 0)
+        if stage == 0:
+            src, dst, there = self.window(self.part, h, False), self.one[h], one
+        elif stage == 1:
+            src, dst, there = self.window(self.part, h, True, False), self.two[h], two
+        elif stage == 2:
+            src, dst, there = self.window(self.part, h, True, True), self.window(self.total, h, True, True), two
+        else:
+            src, dst, there = self.window(self.total, h, True), self.window(self.total, h, True), one
+        return remote(src, dst, self.sends.at[stage, h], self.recvs.at[stage, h], self.nbrs[there], self.e)
+
+    def store(self, h):
+        return pltpu.make_async_copy(
+            self.window(self.part, h, True, True), self.window(self.total, h, True, True), self.store_sem.at[h]
         )
 
-    def hand(self, i):
-        return remote(
-            self.summed, self.rows(self.total, self.c), self.b_send.at[i], self.b_recv.at[i], self.there(i), self.e
-        )
-
-    def handed(self, i):
-        source = lax.rem(self.c + self.size - 1 - i, self.size)
-        return remote(
-            self.summed, self.rows(self.total, source), self.b_send.at[i], self.b_recv.at[i], self.there(i), self.e
-        )
-
-    def store(self):
-        return pltpu.make_async_copy(self.summed, self.rows(self.total, self.c), self.store_sem)
-
     def begin(self):
-        for i in range(self.size - 1):
-            self.give(i).start()
-
-    def middle(self):
-        for i in range(self.size - 1):
-            self.give(i).wait_recv()
-        for j in range(self.piece // 16):
-            at = pl.ds(j * 16, 16)
-            total = self.part[pl.ds(pl.multiple_of(self.c * self.piece + j * 16, 16), 16), :].astype(jnp.float32)
-            for i in range(self.size - 1):
-                total = total + self.arrived_at[i, at, :].astype(jnp.float32)
-            self.summed[at, :] = total.astype(self.summed.dtype)
-        for i in range(self.size - 1):
-            self.hand(i).start()
-        self.store().start()
+        for h in range(2):
+            self.copy(0, h).start()
+
+    def second(self):
+        for h in range(2):
+            self.copy(0, h).wait_recv()
+            kept = self.window(self.part, h, True)
+            add_rows(kept, kept, self.one[h], self.rows // 2)
+            self.copy(1, h).start()
+
+    def third(self):
+        for h in range(2):
+            self.copy(1, h).wait_recv()
+            kept = self.window(self.part, h, True, True)
+            add_rows(kept, kept, self.two[h], self.rows // 4)
+            self.copy(2, h).start()
+            self.store(h).start()
+
+    def fourth(self):
+        for h in range(2):
+            self.store(h).wait()
+            self.copy(2, h).wait_recv()
+            self.copy(3, h).start()
 
     def end(self):
-        self.store().wait()
-        for i in range(self.size - 1):
-            self.give(i).wait_send()
-            self.hand(i).wait_send()
-            self.handed(i).wait_recv()
+        for h in range(2):
+            for stage in range(3):
+                self.copy(stage, h).wait_send()
+            self.copy(3, h).wait()
 
     @staticmethod
-    def scratch(size, rows, width):
+    def scratch(rows, width):
         dma = pltpu.SemaphoreType.DMA
+        wide = [count for _, count in Sharing.columns(width)]
         return [
-            pltpu.VMEM((rows // size, width), jnp.bfloat16),
-            pltpu.VMEM((size - 1, rows // size, width), jnp.bfloat16),
-            dma((size - 1,)),
-            dma((size - 1,)),
-            dma((size - 1,)),
-            dma((size - 1,)),
-            dma,
+            *(pltpu.VMEM((rows // 2, one), jnp.bfloat16) for one in wide),
+            *(pltpu.VMEM((rows // 4, one), jnp.bfloat16) for one in wide),
+            dma((4, 2)),
+            dma((4, 2)),
+            dma((2,)),
         ]
 
 
@@ -662,7 +691,7 @@
 
 
 def planned(size, n, shard_rows):
-    return size == 4 and n in (4, 6, 8) and (shard_rows // 4) % 16 == 0
+    return size == 4 and n == 8 and (shard_rows // 4) % 16 == 0
 
 
 def gather_weights(shards, mask, block, collective_id):
@@ -726,9 +755,12 @@
 def expert_kernel(line, local, cap, hop, start, hidden, own_grads, grads_in, named, router, w_gate, w_up, w_down, *refs):
     hidden_all, out_part, back_part, grads, grads_all = refs[:5]
     if start:
-        early_first, refs = refs[5], refs[:5] + refs[6:]
+        early_first, early_sums, refs = refs[5], refs[6:8], refs[:5] + refs[8:]
     wg, wu, wd, xs, ds, act, dg, du, es, h_buf, y_buf, out_stage, back_stage, in_stage, down_stage = refs[5:20]
     picks, xs_turned, act_turned, gate_kept, refs = *refs[20:24], refs[:20] + refs[24:]
+    if start:
+        crossed, refs = refs[20:22], refs[:20] + refs[22:]
+        hop_sem, refs = refs[-1], refs[:-1]
     w_sem, own_sem, z_send, z_recv, c_send, c_recv, h_sem, y_sem, o_sem, b_sem, s_sem = refs[20:31]
     f32, bf16 = jnp.float32, jnp.bfloat16
     c, e = lax.axis_index("ctx"), lax.axis_index("exp")
@@ -871,6 +903,16 @@
             back_stage[slot, b, :, width : width + lanes] = dot_tn(pick_pair[b], spread).astype(bf16)
         store_out(q, slot).start()
         store_back(q, slot).start()
+
+    at_end = (p == 0) | (p == line - 1)
+
+    def cross_over(n):
+        stage = (back_stage, out_stage)[n]
+        return remote(stage.at[1, 1 - k], crossed[n], hop_sem.at[n, 0], hop_sem.at[n, 1], c, sibling)
+
+    def send_ahead(n):
+        there = jnp.where(p == 0, e + 2, e - 2)
+        return remote(crossed[n], early_sums[n], hop_sem.at[n, 2], hop_sem.at[n, 3], c, there)
 
     def one_chip(i, carried):
         q, d, first = visit(p, line, i)
@@ -957,6 +999,19 @@
         def _():
             pump(d + 1)
 
+        if start:
+            @pl.when(at_end & (i == 1))
+            def _():
+                for n in range(2):
+                    cross_over(n).start()
+
+            @pl.when(at_end & (i == 2))
+            def _():
+                for n, stage in enumerate((back_stage, out_stage)):
+                    cross_over(n).wait()
+                    add_rows(crossed[n], crossed[n], stage.at[1, k], rows)
+                    send_ahead(n).start()
+
         return carried
 
     lax.fori_loop(0, line, one_chip, 0)
@@ -1023,6 +1078,17 @@
 
     if start:
         totals.end_early()
+
+        @pl.when(at_end)
+        def _():
+            for n in range(2):
+                send_ahead(n).wait_send()
+
+        @pl.when((p == 1) | (p == line - 2))
+        def _():
+            for n in range(2):
+                send_ahead(n).wait_recv()
+
     if hop:
         hops.finish([2], [])
     for i in range(max(0, line - 2), line):
@@ -1059,7 +1125,11 @@
     lanes = router.shape[1]
     dma = pltpu.SemaphoreType.DMA
     vmem = pl.BlockSpec(memory_space=pltpu.VMEM)
-    slots = n * cap
+    early = (
+        Totals.early_landing(3 * local * width // Totals.count, units),
+        jax.ShapeDtypeStruct((rows, width + lanes), bf16),
+        jax.ShapeDtypeStruct((rows, width), bf16),
+    )
     return pl.pallas_call(
         functools.partial(expert_kernel, line, local, cap, hop, start),
         out_shape=(
@@ -1069,9 +1139,9 @@
             jax.ShapeDtypeStruct((3 * local * width, units), bf16),
             jax.ShapeDtypeStruct(grads_all.shape, bf16),
         )
-        + ((Totals.early_landing(3 * local * width // Totals.count, units),) if start else ()),
+        + (early if start else ()),
         in_specs=[ANY, ANY, ANY, vmem, vmem, ANY, ANY, ANY],
-        out_specs=(ANY,) * (6 if start else 5),
+        out_specs=(ANY,) * (8 if start else 5),
         input_output_aliases={2: 4},
         scratch_shapes=[
             pltpu.VMEM((local, width, units), bf16),
@@ -1093,6 +1163,9 @@
             pltpu.VMEM((local, width, n * cap), bf16),
             pltpu.VMEM((local, units, n * cap), bf16),
             pltpu.VMEM((2, local * cap, 128), jnp.float32),
+        ]
+        + ([pltpu.VMEM(one.shape, bf16) for one in early[1:]] if start else [])
+        + [
             dma((3,)),
             dma((4,)),
             dma((2, line)),
@@ -1106,7 +1179,7 @@
             dma((2,)),
         ]
         + (Gathering.scratch(line) if hop else [])
-        + (Totals.early_scratch() if start else []),
+        + (Totals.early_scratch() + [dma((2, 4))] if start else []),
         compiler_params=pltpu.CompilerParams(
             collective_id=collective_id, has_side_effects=True, vmem_limit_bytes=62 << 20
         ),
@@ -1311,16 +1384,16 @@
 
 
 def backward_kernel(size, line, heads, kv_heads, experts, fused, *refs):
-    back_part, out_part, grads, early_first, tokens, mid, final, marks, small, gains = refs[:10]
-    queries, keyval, mixed, lse, cosine, sine, qkv_hbm, out_hbm, output, grad_tokens, dense_out, dense_qkv = refs[10:22]
-    refs = refs[22:]
+    back_part, out_part, grads, early_first, early_back, early_out, tokens, mid, final, marks, small, gains = refs[:12]
+    queries, keyval, mixed, lse, cosine, sine, qkv_hbm, out_hbm, output, grad_tokens = refs[12:22]
+    (dense_out, dense_q, dense_kv), refs = refs[22:25], refs[25:]
     if fused:
-        totals, total_out, total_qkv, land_one, land_two = refs[:5]
-        landing, refs = refs[5:13], refs[13:]
+        totals, total_out, total_q, total_kv, land_one, land_two = refs[:6]
+        landing, refs = refs[6:16], refs[16:]
         tmp = refs[0]
-        sum_refs, refs = [refs[1 + 7 * i : 8 + 7 * i] for i in range(4)], refs[29:]
+        sum_refs, refs = [refs[1 + 7 * i : 8 + 7 * i] for i in range(5)], refs[36:]
         total_scratch, refs = refs[:8], refs[8:]
-        share_out, share_qkv, refs = refs[:7], refs[7:14], refs[14:]
+        share_out, share_q, share_kv, refs = refs[:7], refs[7:14], refs[14:21], refs[21:]
     else:
         came, out_sum = back_part, out_part
     wqkv, wout, probs, d_scores, d_mixed, d_att, d_mid, h1, h2, dq, dkv, kv_part, kv_other, stage = refs[:14]
@@ -1357,13 +1430,17 @@
         )
         experts_total.begin()
         sums = [
-            Summing(line, part, landing[2 * i], landing[2 * i + 1], sum_refs[i][0], tmp, sum_refs[i][1:])
-            for i, part in enumerate((back_part, out_part, dense_out, dense_qkv))
+            Summing(
+                line, part, landing[2 * i], landing[2 * i + 1], sum_refs[i][0], tmp, sum_refs[i][1:],
+                (early_back, early_out, None, None, None)[i],
+            )
+            for i, part in enumerate((back_part, out_part, dense_out, dense_q, dense_kv))
         ]
-        back, outs, dense_outs, dense_qkvs = sums
+        back, outs, dense_outs, dense_qs, dense_kvs = sums
         came, out_sum = back.result(), outs.result()
-        sharing_out = Sharing(size, dense_outs.result(), total_out, *share_out[:2], share_out[2:])
-        sharing_qkv = Sharing(size, dense_qkvs.result(), total_qkv, *share_qkv[:2], share_qkv[2:])
+        sharing_out = Sharing(dense_outs.result(), total_out, share_out[:4], share_out[4:])
+        sharing_q = Sharing(dense_qs.result(), total_q, share_q[:4], share_q[4:])
+        sharing_kv = Sharing(dense_kvs.result(), total_kv, share_kv[:4], share_kv[4:])
         back.begin()
     for copy in loads:
         copy.start()
@@ -1512,11 +1589,10 @@
     tick()
     if fused and line > 2:
         dense_outs.step(line - 2)
-    gradients(h1, dq, dense_qkv, 0, q_width // 256)
+    gradients(h1, dq, dense_q, 0, q_width // 256)
+    if fused:
+        dense_qs.begin()
     tick()
-    if fused:
-        for d in range(line - 3, 0, -1):
-            dense_outs.step(d)
 
     own = kv_part[c].astype(f32)
     dkv[...] = own
@@ -1530,7 +1606,10 @@
         dkv[:, at] = turn(dkv[:, at], cosine[...], -sine[...])
     dq[:, q_width:] = dkv[...].astype(bf16)
     dkv_low = dq.at[:, q_width:]
-    gradients(h1, dkv_low, dense_qkv, q_width, 2 * kv_width // 256)
+    gradients(h1, dkv_low, dense_kv, 0, 2 * kv_width // 256)
+    if fused:
+        for d in range(line - 3, 0, -1):
+            dense_outs.step(d)
     loads[0].wait()
 
     def inputs(t, total):
@@ -1550,13 +1629,13 @@
     grad_small = (grad_small + gain_rows.T).astype(bf16).reshape(n, shard, 128)
     stage[0, :, :, 0:128] = grad_small
     small_store = pltpu.make_async_copy(
-        stage.at[0, :, :, 0:128], dense_qkv.at[:, :, q_width + 2 * kv_width :], s_sem.at[0]
+        stage.at[0, :, :, 0:128], dense_kv.at[:, :, 2 * kv_width :], s_sem.at[0]
     )
     small_store.start()
     small_store.wait()
     tick()
     if fused:
-        dense_qkvs.begin()
+        dense_kvs.begin()
 
     def finish(t, carried):
         at = pl.ds(pl.multiple_of(t * 64, 64), 64)
@@ -1565,24 +1644,35 @@
 
     lax.fori_loop(0, rows // 64, finish, 0)
     if fused:
-        tick()
         dense_outs.step(0)
         sharing_out.begin()
+        tick()
         for d in range(line - 2, -1, -1):
+            dense_qs.step(d)
+            if d == 0:
+                sharing_q.begin()
             tick()
-            if d == 0:
-                sharing_out.middle()
-                tick()
-            dense_qkvs.step(d)
-        sharing_qkv.begin()
+            if d == line - 2:
+                sharing_out.second()
+            dense_kvs.step(d)
+            if d == line - 3:
+                sharing_out.third()
+        sharing_kv.begin()
+        sharing_q.second()
+        sharing_out.fourth()
         tick()
-        sharing_qkv.middle()
+        sharing_kv.second()
+        sharing_q.third()
         while len(ticked) < experts_total.ticks:
             tick()
+        sharing_kv.third()
+        sharing_q.fourth()
+        sharing_kv.fourth()
         for one in sums:
             one.end()
         sharing_out.end()
-        sharing_qkv.end()
+        sharing_q.end()
+        sharing_kv.end()
         experts_total.end()
     for i in range(1, size):
         @pl.when(c - i >= 0)
@@ -1590,7 +1680,7 @@
             give(i).wait_send()
 
 
-def backward(experts, shard, back_part, out_part, grads, early_first, tokens, mid, final, marks, small, gains, queries, keyval, mixed, lse,
+def backward(experts, shard, back_part, out_part, grads, early, tokens, mid, final, marks, small, gains, queries, keyval, mixed, lse,
              cosine, sine, qkv_full, out_full, collective_id):
     size, n = lax.axis_size("ctx"), lax.axis_size("exp")
     line = n // 2
@@ -1603,39 +1693,39 @@
     vmem = pl.BlockSpec(memory_space=pltpu.VMEM)
     shape = jax.ShapeDtypeStruct
     fused = planned(size, n, shard)
-    out_width, qkv_width = width, qkv_full.shape[1] + small.shape[1]
+    dense_widths = (width, heads * head, kv_both + small.shape[1])
     shapes = [
         shape((rows, width), bf16),
         shape((rows, width), f32),
-        shape((n, shard, out_width), bf16),
-        shape((n, shard, qkv_width), bf16),
+        *(shape((n, shard, wide), bf16) for wide in dense_widths),
     ]
     summing = []
     if fused:
         deep = grads.shape[0] // Totals.count
         shapes += [
             shape(grads.shape, bf16),
-            shape((shard, out_width), bf16),
-            shape((shard, qkv_width), bf16),
+            *(shape((shard, wide), bf16) for wide in dense_widths),
         ]
         shapes += Totals.landing(deep, grads.shape[1])
-        for high, wide in ((rows, back_part.shape[2]), (rows, width), (shard, out_width), (shard, qkv_width)):
+        summed = [(rows, back_part.shape[2]), (rows, width)] + [(shard, wide) for wide in dense_widths]
+        for high, wide in summed:
             shapes += Summing.landing(line, high, wide)
-        widest = max(back_part.shape[2], width, out_width, qkv_width)
+        widest = max(wide for _, wide in summed)
         summing = [
             pltpu.VMEM((2, rows, widest), bf16),
         ]
-        for high, wide in ((rows, back_part.shape[2]), (rows, width), (shard, out_width), (shard, qkv_width)):
+        for high, wide in summed:
             summing += Summing.scratch(line, high, wide)
         summing += Totals.scratch(deep, grads.shape[1])
-        summing += Sharing.scratch(size, shard, out_width) + Sharing.scratch(size, shard, qkv_width)
+        for wide in dense_widths:
+            summing += Sharing.scratch(shard, wide)
     else:
         back_part = lax.psum_scatter(back_part, "exp", scatter_dimension=0)
         out_part = lax.psum_scatter(out_part, "exp", scatter_dimension=0)
     found = pl.pallas_call(
         functools.partial(backward_kernel, size, line, heads, kv_heads, experts, fused),
         out_shape=tuple(shapes),
-        in_specs=[ANY if fused else vmem] * 2 + [ANY] * 2 + [vmem] * 12 + [ANY] * 2,
+        in_specs=[ANY if fused else vmem] * 2 + [ANY] * 4 + [vmem] * 12 + [ANY] * 2,
         out_specs=(vmem, vmem) + (ANY,) * (len(shapes) - 2),
         scratch_shapes=summing
         + [
@@ -1662,16 +1752,17 @@
             collective_id=collective_id, has_side_effects=True, vmem_limit_bytes=62 << 20
         ),
         name="backward",
-    )(back_part, out_part, grads, early_first, tokens, mid, final, marks, small, gains, queries, keyval, mixed, lse, cosine, sine,
+    )(back_part, out_part, grads, *early, tokens, mid, final, marks, small, gains, queries, keyval, mixed, lse, cosine, sine,
       qkv_full, out_full)
     if fused:
-        return found[:2] + found[4:7]
-    dense_out, dense_qkv = (lax.psum_scatter(part, "exp", scatter_dimension=0) for part in found[2:4])
-    return found[:2] + (lax.psum(grads, "ctx"), lax.psum(dense_out, "ctx"), lax.psum(dense_qkv, "ctx"))
-
-
-def widen_kernel(total, dense_out, dense_qkv, gate, up, down, w_out, w_query, w_keyval, held, held_out, held_qkv, *refs):
-    wide, wide_out, wide_query, wide_keyval, in_sem, out_sem, dense_in, dense_done = refs
+        return found[:2] + found[5:9]
+    dense = tuple(lax.psum_scatter(part, "exp", scatter_dimension=0) for part in found[2:5])
+    return found[:2] + (lax.psum(grads, "ctx"),) + tuple(lax.psum(part, "ctx") for part in dense)
+
+
+def widen_kernel(total, *refs):
+    dense, (gate, up, down), dense_to, held, refs = refs[:3], refs[3:6], refs[6:9], refs[9], refs[10:]
+    held_dense, wide, wide_dense, (in_sem, out_sem, dense_in, dense_done) = refs[:3], refs[3], refs[4:7], refs[7:]
     f32 = jnp.float32
     high = held.shape[1]
     blocks, slots = held.shape[0], wide.shape[0]
@@ -1690,11 +1781,11 @@
 
     small_in = [
         pltpu.make_async_copy(src, dst, dense_in.at[i])
-        for i, (src, dst) in enumerate(((dense_out, held_out), (dense_qkv, held_qkv)))
+        for i, (src, dst) in enumerate(zip(dense, held_dense))
     ]
     small_done = [
         pltpu.make_async_copy(src, dst, dense_done.at[i])
-        for i, (src, dst) in enumerate(((wide_out, w_out), (wide_query, w_query), (wide_keyval, w_keyval)))
+        for i, (src, dst) in enumerate(zip(wide_dense, dense_to))
     ]
     load(0).start()
     for copy in small_in:
@@ -1710,10 +1801,8 @@
         if i == 0:
             for copy in small_in:
                 copy.wait()
-            split = w_query.shape[1]
-            wide_out[...] = held_out[...].astype(f32)
-            wide_query[...] = held_qkv[:, :split].astype(f32)
-            wide_keyval[...] = held_qkv[:, split : split + w_keyval.shape[1]].astype(f32)
+            for src, dst in zip(held_dense, wide_dense):
+                dst[...] = src[:, : dst.shape[1]].astype(f32)
             for copy in small_done:
                 copy.start()
     for i in range(max(0, blocks - slots), blocks):
@@ -1722,13 +1811,12 @@
         copy.wait()
 
 
-def widen(total, dense_out, dense_qkv, local, width, units, q_width, kv_both):
+def widen(total, parts, local, width, units, kv_both):
     f32 = jnp.float32
     blocks, slots = total.shape[0] // units, 4
-    shard = dense_out.shape[0]
     shape = jax.ShapeDtypeStruct
     dma = pltpu.SemaphoreType.DMA
-    dense = [(shard, width), (shard, q_width), (shard, kv_both)]
+    dense = [parts[0].shape, parts[1].shape, (parts[2].shape[0], kv_both)]
     return pl.pallas_call(
         widen_kernel,
         out_shape=(
@@ -1737,22 +1825,21 @@
             shape((local, units, width), f32),
             *(shape(one, f32) for one in dense),
         ),
-        in_specs=[ANY] * 3,
+        in_specs=[ANY] * 4,
         out_specs=(ANY,) * 6,
         scratch_shapes=[
             pltpu.VMEM((blocks, units, units), total.dtype),
-            pltpu.VMEM(dense_out.shape, dense_out.dtype),
-            pltpu.VMEM(dense_qkv.shape, dense_qkv.dtype),
+            *(pltpu.VMEM(one.shape, one.dtype) for one in parts),
             pltpu.VMEM((slots, units, units), f32),
             *(pltpu.VMEM(one, f32) for one in dense),
             dma((blocks,)),
             dma((slots,)),
-            dma((2,)),
+            dma((3,)),
             dma((3,)),
         ],
         compiler_params=pltpu.CompilerParams(vmem_limit_bytes=56 << 20),
         name="widen",
-    )(total, dense_out, dense_qkv)
+    )(total, *parts)
 
 
 def rope_tables(first_row, row_count, head_size):
@@ -1819,16 +1906,16 @@
         hops, experts, tokens[0], small_full, cosine, sine, qkv_full, out_full, rows_all, 2
     )
 
-    _, out_part, back_part, grads, *early_first = expert_pass(
+    _, out_part, back_part, grads, _, *early = expert_pass(
         hops and exp_size > 6, hops, capacity, hidden_two, cotangent[0], rows_all, named, small_full, w_gate, w_up, w_down, 3
     )
-    output, grad_input, grads, dense_out, dense_qkv = backward(
-        experts, shard_rows, back_part, out_part, grads, early_first[-1], tokens[0], resid_mid, cotangent[0], named_own, small_full, gains,
+    output, grad_input, grads, *dense = backward(
+        experts, shard_rows, back_part, out_part, grads, early or [grads] * 3, tokens[0], resid_mid, cotangent[0], named_own, small_full, gains,
         queries, keyval, mixed, lse, cosine, sine, qkv_full, out_full, 4
     )
-    small_total = dense_qkv[:, q_width + 2 * kv_width :].astype(f32)
+    small_total = dense[2][:, 2 * kv_width :].astype(f32)
     grad_gate, grad_up, grad_down, grad_out, grad_query, grad_keyval = widen(
-        grads, dense_out, dense_qkv, local_experts, width, w_gate.shape[2], q_width, 2 * kv_width
+        grads, dense, local_experts, width, w_gate.shape[2], 2 * kv_width
     )
     return (
         output[None],

time: 496 us -> 490 us (0.988)
  Pallas kernels: 475 us -> 469 us
    pallas_call x1, Pallas kernels: 258 us -> 251 us  [backward(): pl.pallas_call(functools.partial(backward_kernel, size, line, heads, kv_h...]
where the time goes in v1:
time: 490 us; the launch traced here: 483 us
  Pallas kernels  469 us (96%)
  other arithmetic  6.61 us (1%)
  local copies, waits for them, and re-layouts  5.89 us (1%)
    pallas_call x1, Pallas kernels, backward(): pl.pallas_call(functools.partial(backward_kernel, size, line, heads, kv_h...  251 us
    pallas_call x1, Pallas kernels, expert_pass(): pl.pallas_call(functools.partial(expert_kernel, line, local, cap, hop, st...  112 us
    pallas_call x1, Pallas kernels, gather_weights(): pl.pallas_call(functools.partial(weights_kernel, line, shards[0].shape[0]...  54.8 us
    pallas_call x1, Pallas kernels, attend(): pl.pallas_call(functools.partial(attend_kernel, size, line, hop, experts,...  35.2 us
    pallas_call x1, Pallas kernels, widen(): pl.pallas_call(widen_kernel, out_shape=(shape((local, width, units), f32)...  15.8 us

profile of v1, /device:TPU:0, one launch (start us, length us, event | category | flops | bytes accessed | tf_op | source)
XLA Modules:
  0.0 482.7 jit_solution(12017029497622947175)
XLA Ops:
  0.7 0.1 pad.7.clone
  0.7 0.9 fusion
  1.7 0.6 convert_element_type.13.refs_3_.refs_9_
  2.3 0.7 broadcast_in_dim.23
  3.1 0.7 broadcast_in_dim.24
  3.8 0.8 copy.33
  4.6 0.7 maximum_maximum_fusion.refs_2_
  5.3 0.5 fusion.1
  5.9 0.8 pad_maximum_fusion.1
  6.7 2.1 pad_maximum_fusion.refs_0_
  8.9 54.8 %gather_weights.1 = (bf16[1536,2048]{1,0:T(8,128)(2,1)}, bf16[1536,1536]{1,0:T(8,128)(2,1)}, bf16[1536,128]{1,0:T(8,128)(2,1)}, bf16[8,256,128]{2,1,0:T(8,128)(2,1)}, bf16[8,256,1536]{2,1,0:T(8,128)(2,1)}) custom-call(bf16[192,2048]{1,0:T(8,128)(2,1)} %pad_maximum_fusion.refs_0_, bf16[192,1536]{1,0:T(8,128)(2,1)} %refs_1_.1, ...), custom_call_target="tpu_custom_call" | custom-call | tf_op jit(solution)/shard_map/gather_weights/pallas_call | solution.py:705
  63.7 35.2 %attend.1 = (bf16[12,256,128]{2,1,0:T(8,128)(2,1)}, bf16[4,256,512]{2,1,0:T(8,128)(2,1)}, bf16[256,1536]{1,0:T(8,128)(2,1)}, f32[256,128]{1,0:T(8,128)}, f32[256...) custom-call(bf16[256,1536]{1,0:T(8,128)(2,1)} %bitcast.9, ...), custom_call_target="tpu_custom_call", output_to_operand_aliasing={{7}: (6, {})} | custom-call | tf_op jit(solution)/shard_map/attend/pallas_call | solution.py:1357
  98.8 112.2 %expert_pass.1 = (bf16[8,256,1536]{2,1,0:T(8,128)(2,1)}, bf16[8,256,1536]{2,1,0:T(8,128)(2,1)}, bf16[8,256,1664]{2,1,0:T(8,128)(2,1)}, bf16[9216,768]{1,0:T(8,12...) custom-call(bf16[256,1536]{1,0:T(8,128)(2,1)} %get-tuple-element.46., ...), custom_call_target="tpu_custom_call", output_to_operand_aliasing={{4}: (2, {})} | custom-call | tf_op jit(solution)/shard_map/expert_pass/pallas_call | solution.py:1133
  211.0 251.0 %backward.1 = (bf16[256,1536]{1,0:T(8,128)(2,1)}, f32[256,1536]{1,0:T(8,128)}, bf16[8,192,1536]{2,1,0:T(8,128)(2,1)}, bf16[8,192,1536]{2,1,0:T(8,128)(2,1)}, bf1...) custom-call(bf16[8,256,1664]{2,1,0:T(8,128)(2,1)} %get-tuple-element, ...), custom_call_target="tpu_custom_call" | custom-call | tf_op jit(solution)/shard_map/backward/pallas_call | solution.py:1725
  462.1 0.8 slice_convert_fusion
  462.9 0.8 slice_reduce_fusion
  463.7 0.7 copy.36
  464.4 0.0 copy-start.1
  464.4 0.0 copy-start
  464.4 15.8 %widen.1 = (f32[2,1536,768]{2,1,0:T(8,128)}, f32[2,1536,768]{2,1,0:T(8,128)}, f32[2,768,1536]{2,1,0:T(8,128)}, f32[192,1536]{1,0:T(8,128)}, f32[192,1536]{1,0:T(8,128)}, /*index=5*/f32[192,512]{1,0:T(8,128)}) custom-call(bf16[9216,768]{1,0:T(8,128)(2,1)} %get-tuple-element.64.total, bf16[192,1536]{1,0:T(8,128)(2,1)} %get-tuple-element.65.refs_0_, ...), custom_call_target="tpu_custom_call" | custom-call | tf_op jit(solution)/shard_map/widen/pallas_call | solution.py:1820
  480.2 0.0 copy-done.1
  480.2 0.9 copy.41
  481.1 0.0 copy-done
  481.1 1.1 copy.42
  (3 shorter events, 0.0 us)
Async XLA Ops:
  464.4 15.8 %copy-start.1 = (bf16[256,1536]{1,0:T(8,128)(2,1)S(1)}, bf16[256,1536]{1,0:T(8,128)(2,1)}, u32[]{:S(2)}) copy-start(bf16[256,1536]{1,0:T(8,128)(2,1)} %get-tuple-element.61) | copy-start | bytes 2359300
  464.4 16.7 %copy-start = (f32[256,1536]{1,0:T(8,128)S(1)}, f32[256,1536]{1,0:T(8,128)}, u32[]{:S(2)}) copy-start(f32[256,1536]{1,0:T(8,128)} %get-tuple-element.62) | copy-start | bytes 4718596

commit v2 on v1

--- a/solution.py
+++ b/solution.py
@@ -548,14 +548,19 @@
 
 def weights_kernel(line, quarter, *refs):
     count = 3
-    own, own_mask, own_block = refs[:count], refs[count], refs[count + 1]
+    own, own_mask, own_block = refs[: count + 1], refs[count + 1], refs[count + 2]
+    refs = refs[1:]
     out, masks, blocks = refs[count + 2 : 2 * count + 2], refs[2 * count + 2], refs[2 * count + 3]
     held, refs = refs[2 * count + 4 : 3 * count + 4], refs[3 * count + 4 :]
     local_sem, own_send, own_recv, z_send, z_recv, xy_send, xy_recv, d_send, d_recv, c_send, c_recv = refs[:-10]
     c, e = lax.axis_index("ctx"), lax.axis_index("exp")
     p, k = e // 2, e % 2
     sibling = e + 1 - 2 * k
-    rows = own[0].shape[0]
+    rows, split = own[0].shape
+    places = (held[0].at[:, 0:split], held[0].at[:, split:], *held[1:])
+    loads = [pltpu.make_async_copy(src, dst, local_sem.at[0, i]) for i, (src, dst) in enumerate(zip(own, places))]
+    for copy in loads:
+        copy.start()
     nbr = (c + 1 - 2 * (c % 2), (c + 2) % 4)
     opposite = 3 - c
     greet(
@@ -575,16 +580,13 @@
         return out[a].at[pl.ds(pl.multiple_of((2 * q + k) * rows + column * quarter, 16), quarter), :]
 
     def own_piece(a):
-        return own[a].at[pl.ds(pl.multiple_of(c * quarter, 16), quarter), :]
-
-    def load(a):
-        return pltpu.make_async_copy(own[a], held[a], local_sem.at[0, a])
+        return held[a].at[pl.ds(pl.multiple_of(c * quarter, 16), quarter), :]
 
     def local(a):
         return pltpu.make_async_copy(held[a], whole(a), local_sem.at[1, a])
 
     def own_across(a):
-        return remote(own[a], whole(a), own_send.at[a], own_recv.at[a], c, sibling)
+        return remote(held[a], whole(a), own_send.at[a], own_recv.at[a], c, sibling)
 
     def along(a, q, src, to_right):
         there = e + 2 if to_right else e - 2
@@ -604,6 +606,8 @@
         block = piece(a, q, column)
         return remote(block, block, c_send.at[q, j, a], c_recv.at[q, j, a], c, sibling)
 
+    for copy in loads:
+        copy.wait()
     arrays = range(count)
     marking = Gathering(line, own_mask, masks, refs[-10:-5])
     gathering = Gathering(line, own_block, blocks, refs[-5:], keep_own=False)
@@ -618,9 +622,6 @@
             along(a, p, own_piece(a), False).start()
     for a in arrays:
         own_across(a).start()
-        load(a).start()
-    for a in arrays:
-        load(a).wait()
         local(a).start()
 
     def ends(d):
@@ -696,21 +697,25 @@
 
 def gather_weights(shards, mask, block, collective_id):
     n = lax.axis_size("exp")
-    if not planned(lax.axis_size("ctx"), n, shards[0].shape[0]):
+    rows, high = shards[0].shape[0], n * shards[0].shape[0]
+    if not planned(lax.axis_size("ctx"), n, rows):
+        shards = (jnp.concatenate(shards[:2], 1), *shards[2:])
         whole = tuple(lax.all_gather(w, "exp", axis=0, tiled=True) for w in shards)
         return whole + (lax.all_gather(mask, "exp", axis=0), gather_rows(block, collective_id))
     line = n // 2
-    count = len(shards)
+    count = len(shards) - 1
+    widths = (shards[0].shape[1] + shards[1].shape[1], *(w.shape[1] for w in shards[2:]))
+    dtype = mask.dtype
     dma = pltpu.SemaphoreType.DMA
     return pl.pallas_call(
-        functools.partial(weights_kernel, line, shards[0].shape[0] // 4),
-        out_shape=tuple(jax.ShapeDtypeStruct((n * w.shape[0], w.shape[1]), w.dtype) for w in shards)
+        functools.partial(weights_kernel, line, rows // 4),
+        out_shape=tuple(jax.ShapeDtypeStruct((high, wide), dtype) for wide in widths)
         + tuple(jax.ShapeDtypeStruct((n,) + w.shape, w.dtype) for w in (mask, block)),
-        in_specs=[ANY] * (count + 2),
+        in_specs=[ANY] * (count + 3),
         out_specs=(ANY,) * (count + 2),
-        scratch_shapes=[pltpu.VMEM(w.shape, w.dtype) for w in shards]
+        scratch_shapes=[pltpu.VMEM((rows, wide), dtype) for wide in widths]
         + [
-            dma((2, count)),
+            dma((2, count + 1)),
             dma((count,)),
             dma((count,)),
             dma((2, line, count)),
@@ -1479,6 +1484,7 @@
         tick()
         if fused and d == 2:
             outs.begin()
+            tick()
     if fused:
         back.step(0)
         tick()
@@ -1886,7 +1892,7 @@
     scaling = 1.0 / math.sqrt(head)
     first_row = ctx_index * rows
 
-    named_own = jnp.any(routes[0][:, :, None] == jnp.arange(128, dtype=jnp.int32), axis=1).astype(bf16)
+    named_own = jnp.max((routes[0][:, :, None] == jnp.arange(128, dtype=jnp.int32)).astype(bf16), axis=1)
     small = jnp.concatenate(
         [
             w_router,
@@ -1897,7 +1903,7 @@
         1,
     )
     qkv_full, out_full, small_full, named, rows_all = gather_weights(
-        (jnp.concatenate([w_query, key_value_weight], 1), w_out, small), named_own, cotangent[0], 1
+        (w_query, key_value_weight, w_out, small), named_own, cotangent[0], 1
     )
 
     cosine, sine = rope_tables(first_row, rows, head)

time: 490 us -> 486 us (level)
  no operation moved by 1% of the time
where the time goes in v2:
time: 486 us; the launch traced here: 479 us
  Pallas kernels  467 us (96%)
  local copies, waits for them, and re-layouts  5.9 us (1%)
    pallas_call x1, Pallas kernels, backward(): pl.pallas_call(functools.partial(backward_kernel, size, line, heads, kv_h...  249 us
    pallas_call x1, Pallas kernels, expert_pass(): pl.pallas_call(functools.partial(expert_kernel, line, local, cap, hop, st...  112 us
    pallas_call x1, Pallas kernels, gather_weights(): pl.pallas_call(functools.partial(weights_kernel, line, rows // 4), out_sh...  54.8 us
    pallas_call x1, Pallas kernels, attend(): pl.pallas_call(functools.partial(attend_kernel, size, line, hop, experts,...  35.3 us
    pallas_call x1, Pallas kernels, widen(): pl.pallas_call(widen_kernel, out_shape=(shape((local, width, units), f32)...  15.8 us

profile of v2, /device:TPU:0, one launch (start us, length us, event | category | flops | bytes accessed | tf_op | source)
XLA Modules:
  0.0 478.8 jit_solution(6402230937806739372)
XLA Ops:
  0.7 0.1 pad.7.clone
  0.8 0.7 broadcast_in_dim.23
  1.5 0.7 broadcast_in_dim.24
  2.3 0.8 copy.33
  3.1 0.7 maximum_maximum_fusion.refs_3_
  3.8 1.5 fusion.1.refs_4_.refs_9_
  5.3 0.5 fusion.2
  5.9 0.8 pad_maximum_fusion
  6.7 54.8 %gather_weights.1 = (bf16[1536,2048]{1,0:T(8,128)(2,1)}, bf16[1536,1536]{1,0:T(8,128)(2,1)}, bf16[1536,128]{1,0:T(8,128)(2,1)}, bf16[8,256,128]{2,1,0:T(8,128)(2,1)}, bf16[8,256,1536]{2,1,0:T(8,128)(2,1)}) custom-call(bf16[192,1536]{1,0:T(8,128)(2,1)} %refs_0_.1, bf16[192,512]{1,0:T(8,128)(2,1)} %refs_1_.1, bf16[192,1536]{1,0:T(8,128)(2,1)} %refs_2_.1, ...), custom_call_target="tpu_custom_call" | custom-call | tf_op jit(solution)/shard_map/gather_weights/pallas_call | solution.py:710
  61.5 35.3 %attend.1 = (bf16[12,256,128]{2,1,0:T(8,128)(2,1)}, bf16[4,256,512]{2,1,0:T(8,128)(2,1)}, bf16[256,1536]{1,0:T(8,128)(2,1)}, f32[256,128]{1,0:T(8,128)}, f32[256...) custom-call(bf16[256,1536]{1,0:T(8,128)(2,1)} %bitcast.9, ...), custom_call_target="tpu_custom_call", output_to_operand_aliasing={{7}: (6, {})} | custom-call | tf_op jit(solution)/shard_map/attend/pallas_call | solution.py:1362
  96.8 112.2 %expert_pass.1 = (bf16[8,256,1536]{2,1,0:T(8,128)(2,1)}, bf16[8,256,1536]{2,1,0:T(8,128)(2,1)}, bf16[8,256,1664]{2,1,0:T(8,128)(2,1)}, bf16[9216,768]{1,0:T(8,12...) custom-call(bf16[256,1536]{1,0:T(8,128)(2,1)} %get-tuple-element.46., ...), custom_call_target="tpu_custom_call", output_to_operand_aliasing={{4}: (2, {})} | custom-call | tf_op jit(solution)/shard_map/expert_pass/pallas_call | solution.py:1138
  209.0 249.2 %backward.1 = (bf16[256,1536]{1,0:T(8,128)(2,1)}, f32[256,1536]{1,0:T(8,128)}, bf16[8,192,1536]{2,1,0:T(8,128)(2,1)}, bf16[8,192,1536]{2,1,0:T(8,128)(2,1)}, bf1...) custom-call(bf16[8,256,1664]{2,1,0:T(8,128)(2,1)} %get-tuple-element, ...), custom_call_target="tpu_custom_call" | custom-call | tf_op jit(solution)/shard_map/backward/pallas_call | solution.py:1731
  458.2 0.8 slice_convert_fusion
  459.0 0.8 slice_reduce_fusion
  459.8 0.7 copy.36
  460.5 0.0 copy-start.1
  460.5 0.0 copy-start
  460.5 15.8 %widen.1 = (f32[2,1536,768]{2,1,0:T(8,128)}, f32[2,1536,768]{2,1,0:T(8,128)}, f32[2,768,1536]{2,1,0:T(8,128)}, f32[192,1536]{1,0:T(8,128)}, f32[192,1536]{1,0:T(8,128)}, /*index=5*/f32[192,512]{1,0:T(8,128)}) custom-call(bf16[9216,768]{1,0:T(8,128)(2,1)} %get-tuple-element.64.total, bf16[192,1536]{1,0:T(8,128)(2,1)} %get-tuple-element.65.refs_0_, ...), custom_call_target="tpu_custom_call" | custom-call | tf_op jit(solution)/shard_map/widen/pallas_call | solution.py:1826
  476.3 0.0 copy-done.1
  476.3 0.9 copy.41
  477.2 0.0 copy-done
  477.2 1.1 copy.42
  (3 shorter events, 0.0 us)
Async XLA Ops:
  460.5 15.8 %copy-start.1 = (bf16[256,1536]{1,0:T(8,128)(2,1)S(1)}, bf16[256,1536]{1,0:T(8,128)(2,1)}, u32[]{:S(2)}) copy-start(bf16[256,1536]{1,0:T(8,128)(2,1)} %get-tuple-element.61) | copy-start | bytes 2359300
  460.5 16.7 %copy-start = (f32[256,1536]{1,0:T(8,128)S(1)}, f32[256,1536]{1,0:T(8,128)}, u32[]{:S(2)}) copy-start(f32[256,1536]{1,0:T(8,128)} %get-tuple-element.62) | copy-start | bytes 4718596

commit v3 on v2

--- a/solution.py
+++ b/solution.py
@@ -1893,15 +1893,10 @@
     first_row = ctx_index * rows
 
     named_own = jnp.max((routes[0][:, :, None] == jnp.arange(128, dtype=jnp.int32)).astype(bf16), axis=1)
-    small = jnp.concatenate(
-        [
-            w_router,
-            gain_attn[:, None],
-            gain_ffn[:, None],
-            jnp.zeros((shard_rows, 128 - experts - 2), bf16),
-        ],
-        1,
-    )
+    lane = lax.broadcasted_iota(jnp.int32, (shard_rows, 128), 1)
+    gains_wide = [lax.broadcast_in_dim(gain, (shard_rows, 128), (0,)) for gain in (gain_attn, gain_ffn)]
+    small = lax.pad(w_router, jnp.zeros((), bf16), ((0, 0, 0), (0, 128 - experts, 0)))
+    small = jnp.where(lane == experts, gains_wide[0], jnp.where(lane == experts + 1, gains_wide[1], small))
     qkv_full, out_full, small_full, named, rows_all = gather_weights(
         (w_query, key_value_weight, w_out, small), named_own, cotangent[0], 1
     )

time: 486 us -> 485 us (level)
  no operation moved by 1% of the time
where the time goes in v3:
time: 485 us; the launch traced here: 478 us
  Pallas kernels  467 us (96%)
  other arithmetic  5.15 us (1%)
    pallas_call x1, Pallas kernels, backward(): pl.pallas_call(functools.partial(backward_kernel, size, line, heads, kv_h...  249 us
    pallas_call x1, Pallas kernels, expert_pass(): pl.pallas_call(functools.partial(expert_kernel, line, local, cap, hop, st...  112 us
    pallas_call x1, Pallas kernels, gather_weights(): pl.pallas_call(functools.partial(weights_kernel, line, rows // 4), out_sh...  54.8 us
    pallas_call x1, Pallas kernels, attend(): pl.pallas_call(functools.partial(attend_kernel, size, line, hop, experts,...  35.3 us
    pallas_call x1, Pallas kernels, widen(): pl.pallas_call(widen_kernel, out_shape=(shape((local, width, units), f32)...  15.8 us

profile of v3, /device:TPU:0, one launch (start us, length us, event | category | flops | bytes accessed | tf_op | source)
XLA Modules:
  0.0 477.9 jit_solution(14080111212790949648)
XLA Ops:
  0.7 0.8 copy.31
  1.5 1.4 select_select_fusion.refs_3_
  2.9 1.5 fusion.1.refs_4_.refs_9_
  4.5 0.5 fusion.2
  5.0 0.8 pad_maximum_fusion
  5.8 54.8 %gather_weights.1 = (bf16[1536,2048]{1,0:T(8,128)(2,1)}, bf16[1536,1536]{1,0:T(8,128)(2,1)}, bf16[1536,128]{1,0:T(8,128)(2,1)}, bf16[8,256,128]{2,1,0:T(8,128)(2,1)}, bf16[8,256,1536]{2,1,0:T(8,128)(2,1)}) custom-call(bf16[192,1536]{1,0:T(8,128)(2,1)} %refs_0_.1, bf16[192,512]{1,0:T(8,128)(2,1)} %refs_1_.1, bf16[192,1536]{1,0:T(8,128)(2,1)} %refs_2_.1, ...), custom_call_target="tpu_custom_call" | custom-call | tf_op jit(solution)/shard_map/gather_weights/pallas_call | solution.py:710
  60.7 35.3 %attend.1 = (bf16[12,256,128]{2,1,0:T(8,128)(2,1)}, bf16[4,256,512]{2,1,0:T(8,128)(2,1)}, bf16[256,1536]{1,0:T(8,128)(2,1)}, f32[256,128]{1,0:T(8,128)}, f32[256...) custom-call(bf16[256,1536]{1,0:T(8,128)(2,1)} %bitcast.9, ...), custom_call_target="tpu_custom_call", output_to_operand_aliasing={{7}: (6, {})} | custom-call | tf_op jit(solution)/shard_map/attend/pallas_call | solution.py:1362
  95.9 112.2 %expert_pass.1 = (bf16[8,256,1536]{2,1,0:T(8,128)(2,1)}, bf16[8,256,1536]{2,1,0:T(8,128)(2,1)}, bf16[8,256,1664]{2,1,0:T(8,128)(2,1)}, bf16[9216,768]{1,0:T(8,12...) custom-call(bf16[256,1536]{1,0:T(8,128)(2,1)} %get-tuple-element.46., ...), custom_call_target="tpu_custom_call", output_to_operand_aliasing={{4}: (2, {})} | custom-call | tf_op jit(solution)/shard_map/expert_pass/pallas_call | solution.py:1138
  208.2 249.2 %backward.1 = (bf16[256,1536]{1,0:T(8,128)(2,1)}, f32[256,1536]{1,0:T(8,128)}, bf16[8,192,1536]{2,1,0:T(8,128)(2,1)}, bf16[8,192,1536]{2,1,0:T(8,128)(2,1)}, bf1...) custom-call(bf16[8,256,1664]{2,1,0:T(8,128)(2,1)} %get-tuple-element, ...), custom_call_target="tpu_custom_call" | custom-call | tf_op jit(solution)/shard_map/backward/pallas_call | solution.py:1731
  457.4 0.8 slice_convert_fusion
  458.2 0.8 slice_reduce_fusion
  459.0 0.7 copy.32
  459.6 0.0 copy-start.1
  459.7 0.0 copy-start
  459.7 15.8 %widen.1 = (f32[2,1536,768]{2,1,0:T(8,128)}, f32[2,1536,768]{2,1,0:T(8,128)}, f32[2,768,1536]{2,1,0:T(8,128)}, f32[192,1536]{1,0:T(8,128)}, f32[192,1536]{1,0:T(8,128)}, /*index=5*/f32[192,512]{1,0:T(8,128)}) custom-call(bf16[9216,768]{1,0:T(8,128)(2,1)} %get-tuple-element.64.total, bf16[192,1536]{1,0:T(8,128)(2,1)} %get-tuple-element.65.refs_0_, ...), custom_call_target="tpu_custom_call" | custom-call | tf_op jit(solution)/shard_map/widen/pallas_call | solution.py:1826
  475.5 0.0 copy-done.1
  475.5 0.9 copy.37
  476.4 0.0 copy-done
  476.4 1.1 copy.38
  (3 shorter events, 0.0 us)
Async XLA Ops:
  459.6 15.8 %copy-start.1 = (bf16[256,1536]{1,0:T(8,128)(2,1)S(1)}, bf16[256,1536]{1,0:T(8,128)(2,1)}, u32[]{:S(2)}) copy-start(bf16[256,1536]{1,0:T(8,128)(2,1)} %get-tuple-element.61) | copy-start | bytes 2359300
  459.7 16.7 %copy-start = (f32[256,1536]{1,0:T(8,128)S(1)}, f32[256,1536]{1,0:T(8,128)}, u32[]{:S(2)}) copy-start(f32[256,1536]{1,0:T(8,128)} %get-tuple-element.62) | copy-start | bytes 4718596
